TPU v7x, 512 devices: a whole 4x4x16 slice. The times are simulated.
512 devices in a mesh: frame: 16 (over y, x), tile: 32 (over z, core).
Axes of the slice: x: 4, y: 4, z: 16, core: 2. Of those that a mesh axis runs over, the one named last changes fastest.
Arguments:
- features: bfloat16 [32, 192, 64, 128], P('frame', 'tile'), may hold values from -40 to 40
- norm_gain_weight: float32 [128], replicated, may hold values from 0.5 to 2
- norm_bias: float32 [128], replicated, may hold values from -1 to 1
- kernel: bfloat16 [3, 3, 3, 128, 128], replicated, may hold values from -0.109375 to 0.109375
- cotangent: bfloat16 [32, 192, 64, 128], P('frame', 'tile'), may hold values from -6 to 6
Outputs:
- feature_gradient: bfloat16 [32, 192, 64, 128], P('frame', 'tile')
- grad_kernel: float32 [3, 3, 3, 128, 128], replicated
- gain_gradient: float32 [128], replicated
- grad_shift: float32 [128], replicated
All inputs are finite; a program needn't handle non-finite values.
Results may differ from a plain program's by a relative error of at most 0.0012.
The roundings to bfloat16 on the way count: a program that leaves them out, or rounds other values in their place, can miss the bound.
Values may be sent and summed in bfloat16 or wider, within the bound.
A program may use at most 64 MiB of HBM per device.

v0:
```python
import jax
import jax.numpy as jnp
from jax import lax
from jax.sharding import PartitionSpec as P

GROUPS = 32


epsilon = 1e-06


def padded(cells, sides, width):
    for axis, dim in sides:
        count = lax.axis_size(axis)
        ends = count - 1
        head = lax.slice_in_dim(cells, 0, width, axis=dim)
        tail = lax.slice_in_dim(cells, cells.shape[dim] - width, cells.shape[dim], axis=dim)
        cells = jnp.concatenate(
            [
                lax.ppermute(tail, axis, [(i, (i + 1) % count) for i in range(ends)]),
                cells,
                lax.ppermute(head, axis, [((i + 1) % count, i) for i in range(ends)]),
            ],
            axis=dim,
        )
    return cells


def shifted(block, axis, distance):
    devices = range(lax.axis_size(axis))
    route = [(i - distance, i) for i in devices if i - distance in devices]
    return lax.ppermute(block, axis, route)


def apply_group_norm(
    block_region, average, inverse_deviation, norm_gain_weight, norm_bias, per_group
):
    grouped = block_region.astype(jnp.float32).reshape(-1, GROUPS, per_group)
    centered_values = grouped - average[None, :, None]
    standardized_input = (centered_values * inverse_deviation[None, :, None]).reshape(
        block_region.shape
    )
    normed_output = standardized_input * norm_gain_weight + norm_bias
    sigmoid_output = jax.nn.sigmoid(normed_output)
    return (standardized_input, normed_output, sigmoid_output)


def on_device(features, norm_gain_weight, norm_bias, kernel, cotangent):
    frames, height, across, channels = features.shape
    per_group = channels // GROUPS
    cell_count = (
        frames * height * across * per_group * lax.axis_size("frame") * lax.axis_size("tile")
    )
    value_array = features.astype(jnp.float32)
    grouped = value_array.reshape(-1, GROUPS, per_group)
    average = lax.psum(jnp.sum(grouped, axis=(0, 2)), ("frame", "tile")) / cell_count
    centered_values = grouped - average[None, :, None]
    spread = (
        lax.psum(jnp.sum(centered_values * centered_values, axis=(0, 2)), ("frame", "tile"))
        / cell_count
    )
    inverse_deviation = lax.rsqrt(spread + epsilon)
    standardized_input, normed_output, sigmoid_output = apply_group_norm(
        features, average, inverse_deviation, norm_gain_weight, norm_bias, per_group
    )
    activated = (normed_output * sigmoid_output).astype(jnp.bfloat16)
    act_rows = padded(activated, (("tile", 1),), 1)
    earlier = shifted(act_rows, "frame", 1)
    act_full = jnp.pad(
        jnp.concatenate([earlier, act_rows], axis=0), ((0, 0), (0, 0), (1, 1), (0, 0))
    )
    grad_rows = padded(cotangent, (("tile", 1),), 1)
    following = shifted(grad_rows, "frame", -1)
    grad_full = jnp.pad(
        jnp.concatenate([grad_rows, following], axis=0), ((0, 0), (0, 0), (1, 1), (0, 0))
    )
    grad_flat = cotangent.reshape(-1, channels)
    grad_act = jnp.zeros((grad_flat.shape[0], channels), jnp.float32)
    kernel_rows = []
    for frame_tap in range(3):
        for row_tap in range(3):
            patches = jnp.concatenate(
                [
                    act_full[
                        frame_tap : frame_tap + frames,
                        row_tap : row_tap + height,
                        col_tap : col_tap + across,
                    ]
                    for col_tap in range(3)
                ],
                axis=-1,
            ).reshape(-1, 3 * channels)
            kernel_rows.append(
                lax.dot_general(
                    patches, grad_flat, (((0,), (0,)), ((), ())), preferred_element_type=jnp.float32
                ).reshape(3, channels, channels)
            )
            back_patches = jnp.concatenate(
                [
                    grad_full[
                        2 - frame_tap : 2 - frame_tap + frames,
                        2 - row_tap : 2 - row_tap + height,
                        2 - col_tap : 2 - col_tap + across,
                    ]
                    for col_tap in range(3)
                ],
                axis=-1,
            ).reshape(-1, 3 * channels)
            tap_matrix = jnp.transpose(kernel[frame_tap, row_tap], (0, 2, 1)).reshape(
                3 * channels, channels
            )
            grad_act = grad_act + jnp.dot(
                back_patches, tap_matrix, preferred_element_type=jnp.float32
            )
    local_kernel = jnp.stack(kernel_rows).reshape(3, 3, 3, channels, channels)
    normed_gradient = (
        grad_act.reshape(value_array.shape)
        * sigmoid_output
        * (1.0 + normed_output * (1.0 - sigmoid_output))
    )
    shard_gain = jnp.sum(normed_gradient * standardized_input, axis=(0, 1, 2))
    local_shift = jnp.sum(normed_gradient, axis=(0, 1, 2))
    grad_kernel = lax.psum(local_kernel, ("frame", "tile"))
    gain_gradient, grad_shift = lax.psum((shard_gain, local_shift), ("frame", "tile"))
    grad_mean = (
        jnp.sum((norm_gain_weight * grad_shift).reshape(GROUPS, per_group), axis=1) / cell_count
    )
    grad_proj = (
        jnp.sum((norm_gain_weight * gain_gradient).reshape(GROUPS, per_group), axis=1) / cell_count
    )
    channel_mean = jnp.repeat(grad_mean, per_group)
    channel_projection = jnp.repeat(grad_proj, per_group)
    inverse_channel_count = jnp.repeat(inverse_deviation, per_group)
    feature_gradient = (
        inverse_channel_count
        * (
            normed_gradient * norm_gain_weight
            - channel_mean
            - standardized_input * channel_projection
        )
    ).astype(jnp.bfloat16)
    return (feature_gradient, grad_kernel, gain_gradient, grad_shift)


def solution(mesh):
    placed = (P("frame", "tile", None, None), P(), P(), P(), P("frame", "tile", None, None))
    return jax.shard_map(
        on_device,
        mesh=mesh,
        in_specs=placed,
        out_specs=(P("frame", "tile", None, None), P(), P(), P()),
        check_vma=False,
    )
```

profile of v0, /device:TPU:1, one launch (start us, length us, event | category | flops | bytes accessed | tf_op | source)
XLA Modules:
  0.0 861.6 jit_solution(2107972409060627535)
XLA Ops:
  9.3 4.9 collective-permute-start
  14.3 109.3 %psum.35 = f32[32]{0:T(128)S(1)} all-reduce(f32[32]{0:T(128)S(1)} %reduce_sum.70), channel_id=1, replica_groups=mesh['frame'=16,'tile'=32] {'frame','tile'}, use_global_device_ids=true, to_apply=%region_2.0 | all-reduce | flops 32 | bytes 256 | tf_op jit(solution)/shard_map/psum | solution.py:56
  125.0 2.7 collective-permute-start.1
  127.8 98.7 %psum.36 = f32[32]{0:T(128)S(1)} all-reduce(f32[32]{0:T(128)S(1)} %reduce_sum.73), channel_id=1, replica_groups=mesh['frame'=16,'tile'=32] {'frame','tile'}, use_global_device_ids=true, to_apply=%region_5.6 | all-reduce | flops 32 | bytes 256 | tf_op jit(solution)/shard_map/psum | solution.py:59
  227.5 1.3 collective-permute-start.2
  230.3 6.3 collective-permute-done.2
  243.5 3.5 collective-permute-start.4
  247.0 3.6 collective-permute-start.3
  251.6 1.9 collective-permute-start.5
  253.5 102.7 %all-reduce.2 = (f32[128]{0:T(128)S(1)}, f32[128]{0:T(128)}) all-reduce(f32[128]{0:T(128)S(1)} %get-tuple-element.5, f32[128]{0:T(128)S(1)} %get-tuple-element.4), channel_id=1, replica_groups=mesh['frame'=16,'tile'=32] {'frame','tile'}, use_global_device_ids=true, to_apply=%region_10.11 | all-reduce | flops 256 | bytes 2048 | tf_op jit(solution)/shard_map/psum | solution.py:124
  356.2 1.3 pad_slice_fusion.7
  357.6 1.4 pad_slice_fusion.6
  360.9 1.2 pad_maximum_fusion.15
  362.4 2.0 pad_maximum_fusion.16
  364.4 1.3 copy.31
  365.7 2.0 pad_maximum_fusion.17
  367.7 2.1 copy.32
  369.8 2.7 fusion.10
  372.5 2.1 copy.33
  374.6 2.2 copy.34
  376.8 2.1 copy.35
  382.7 1.2 copy-done.6
  385.7 466.2 %all-reduce.5.cloned.1.call-done = f32[3,3,3,128,128]{4,3,2,1,0:T(8,128)} async-done(((f32[3,3,3,128,128]{4,3,2,1,0:T(8,128)}), f32[3,3,3,128,128]{4,3,2,1,0:T(8,128)}) %all-reduce.5.cloned.1.call-update) | async-done | bytes 1769488 | tf_op jit(solution)/shard_map/psum | solution.py:123
  851.9 2.9 copy.56
  (115 shorter events, 21.3 us)
Async XLA Ops:
  7.2 221.8 %copy-start.8 = (bf16[3,3,3,128,128]{4,3,2,1,0:T(8,128)(2,1)S(1)}, bf16[3,3,3,128,128]{4,3,2,1,0:T(8,128)(2,1)}, u32[]{:S(2)}) copy-start(bf16[3,3,3,128,128]{4,3,2,1,0:T(8,128)(2,1)} %param.8) | copy-start | bytes 2654212
  7.2 844.7 %all-reduce.5.cloned.1.call-start = ((), (), s32[]{:S(2)}) async-start(), calls=%async_computation | async-start | bytes 3538944 | tf_op jit(solution)/shard_map/psum | solution.py:123
  9.3 217.2 %collective-permute-start = (bf16[2,1,64,128]{3,2,1,0:T(8,128)(2,1)S(1)}, bf16[2,1,64,128]{3,2,1,0:T(8,128)(2,1)S(1)}, u32[]{:S(2)}, u32[]{:S(2)}) collective-permute-start(bf16[2,1,64,128]{3,2,1,0:T(8,128)(2,1)S(1)} %get-tuple-element.75), channel_id=1, source_target_pairs={{0,1},{1,2},{2,3},{3,4},{4,5},{5,6},{6,7},{7,8},{8,9},{9,10},{10,1... | collective-permute-start | bytes 98312 | tf_op jit(solution)/shard_map/ppermute | solution.py:20
  125.0 102.4 %collective-permute-start.1 = (bf16[2,1,64,128]{3,2,1,0:T(8,128)(2,1)S(1)}, bf16[2,1,64,128]{3,2,1,0:T(8,128)(2,1)S(1)}, u32[]{:S(2)}, u32[]{:S(2)}) collective-permute-start(bf16[2,1,64,128]{3,2,1,0:T(8,128)(2,1)S(1)} %get-tuple-element.74), channel_id=1, source_target_pairs={{1,0},{2,1},{3,2},{4,3},{5,4},{6,5},{7,6},{8,7},{9,8},{10,9},{11,1... | collective-permute-start | bytes 98312 | tf_op jit(solution)/shard_map/ppermute | solution.py:22
  227.5 9.1 %collective-permute-start.2 = (bf16[2,8,64,128]{3,2,1,0:T(8,128)(2,1)S(1)}, bf16[2,8,64,128]{3,2,1,0:T(8,128)(2,1)S(1)}, u32[]{:S(2)}, u32[]{:S(2)}) collective-permute-start(bf16[2,8,64,128]{3,2,1,0:T(8,128)(2,1)S(1)} %constant_dynamic-update-slice_fusion), channel_id=1, source_target_pairs={{32,0},{64,32},{96,64},{128,96},{160,128},{192,160},{224,192},{256... | collective-permute-start | bytes 786440 | tf_op jit(solution)/shard_map/ppermute | solution.py:32
  237.6 0.9 copy-start
  241.6 0.9 copy-start.1
  241.6 0.9 copy-start.12
  241.6 0.9 copy-start.13
  243.5 7.1 collective-permute-start.4
  247.0 4.6 collective-permute-start.3
  250.6 107.0 %copy-start.10 = (bf16[2,1,64,128]{3,2,1,0:T(8,128)(2,1)}, bf16[2,1,64,128]{3,2,1,0:T(8,128)(2,1)S(1)}, u32[]{:S(2)}) copy-start(bf16[2,1,64,128]{3,2,1,0:T(8,128)(2,1)S(1)} %collective-permute-done.4) | copy-start | bytes 98308
  251.6 106.0 %copy-start.11 = (bf16[2,1,64,128]{3,2,1,0:T(8,128)(2,1)}, bf16[2,1,64,128]{3,2,1,0:T(8,128)(2,1)S(1)}, u32[]{:S(2)}) copy-start(bf16[2,1,64,128]{3,2,1,0:T(8,128)(2,1)S(1)} %collective-permute-done.3) | copy-start | bytes 98308
  251.6 104.6 %collective-permute-start.5 = (bf16[2,8,64,128]{3,2,1,0:T(8,128)(2,1)S(1)}, bf16[2,8,64,128]{3,2,1,0:T(8,128)(2,1)S(1)}, u32[]{:S(2)}, u32[]{:S(2)}) collective-permute-start(bf16[2,8,64,128]{3,2,1,0:T(8,128)(2,1)S(1)} %pad_maximum_fusion.19), channel_id=1, source_target_pairs={{0,32},{32,64},{64,96},{96,128},{128,160},{160,192},{192,224},{224... | collective-permute-start | bytes 786440 | tf_op jit(solution)/shard_map/ppermute | solution.py:32
  356.2 27.8 %copy-start.14 = (f32[128]{0:T(128)}, f32[128]{0:T(128)S(1)}, u32[]{:S(2)}) copy-start(f32[128]{0:T(128)S(1)} %get-tuple-element.85) | copy-start | bytes 1540
  359.3 0.9 copy-start.9
  379.9 1.1 copy-start.2
  380.2 1.1 copy-start.5
  380.5 1.2 copy-start.3
  381.3 1.1 copy-start.4
  382.4 1.6 copy-start.15
  382.7 1.2 copy-start.6
  383.9 1.0 copy-start.7
Sparse Core Ops, SparseCore 0:
  384.1 467.7 all-reduce.4
where the time goes:
time: 863 us; the launch traced here: 862 us
  waiting for transfers between devices  473 us (55%)
  blocking collectives  311 us (36%)
  local copies, waits for them, and re-layouts  25.6 us (3%)
  starting transfers between devices  18 us (2%)
  between operations  14.7 us (2%)
  other arithmetic  13.6 us (2%)
    psum x1, waiting for transfers between devices, on_device(): grad_kernel = lax.psum(local_kernel, ('frame', 'tile'))  466 us
    psum x1, blocking collectives, on_device(): lax.psum(jnp.sum(grouped, axis=(0, 2)), ('frame', 'tile')) / cell_count  109 us
    psum x1, blocking collectives, on_device(): lax.psum((shard_gain, local_shift), ('frame', 'tile'))  103 us
    psum x1, blocking collectives, on_device(): lax.psum(jnp.sum(centered_values * centered_values, axis=(0, 2)), ('frame...  98.7 us
  transfers between devices with their start and end apart: 7, of which 3 were waited for; matrix products, arithmetic and copies ran while one was open for 1% of the time, Pallas kernels for 0%

commit v1 on v0

v1 whole, which is shorter than its diff:
```python
import jax
import jax.numpy as jnp
from jax import lax
from jax.experimental import pallas as pl
from jax.experimental.pallas import tpu as pltpu
from jax.sharding import PartitionSpec as P

MESH = pl.DeviceIdType.MESH
GROUPS = 32
EPS = 1e-06
NX = 4
NY = 4
NZ = 16
TAPS = 28
TY = TAPS // NY
NTILES = 2 * TY
F32 = jnp.float32
BF16 = jnp.bfloat16


def group_sum(v):
    lane = lax.broadcasted_iota(jnp.int32, v.shape, 1)
    v = v + jnp.where(lane % 2 == 0, pltpu.roll(v, 127, 1), pltpu.roll(v, 1, 1))
    return v + jnp.where(lane % 4 < 2, pltpu.roll(v, 126, 1), pltpu.roll(v, 2, 1))


def body(
    feat, gain, bias, w, cot,
    fg, gk, gs,
    ext, cotx, gact, xhat, act_t, s1, s2, g1, g2,
    part, rc, ra1, rb1, ra2, rb2, zsrc, rz, zg,
    halo_s, halo_r, s1_s, s1_r, s2_s, s2_r, g1_s, g1_r, g2_s, g2_r,
    core_s, core_r, st_s, st_r, z_s, z_r, zg_s, zg_r, ag_s, ag_r,
):
    f, t = lax.axis_index("frame"), lax.axis_index("tile")
    nf, nt = NX * NY, NZ * 2
    y, x = f // NX, f % NX
    z, core = t // 2, t % 2
    frames, rows, cols, ch = feat.shape
    cells = frames * rows * cols
    chunk = 128
    barrier = pltpu.get_barrier_semaphore()

    def at(df, dt):
        return ((f + df + nf) % nf, (t + dt + nt) % nt)

    def rcopy(src, dst, ss, rs, dev):
        return pltpu.make_async_remote_copy(
            src_ref=src, dst_ref=dst, send_sem=ss, recv_sem=rs,
            device_id=dev, device_id_type=MESH,
        )

    def hello(dev):
        pl.semaphore_signal(barrier, inc=1, device_id=dev, device_id_type=MESH)

    @pl.loop(1, nf)
    def _(i):
        hello(((f + i) % nf, t))

    @pl.loop(1, nt)
    def _(i):
        hello((f, (t + i) % nt))

    for df in (-1, 1):
        for dt in (-1, 1):
            hello(at(df, dt))

    def rows_of(ref, k):
        per = cols
        return ref

    flat = feat.reshape(cells, ch)
    flat_cot = cot.reshape(cells, ch)

    def add_up(k, acc):
        return acc + jnp.sum(flat[pl.ds(k * chunk, chunk), :].astype(F32), axis=0, keepdims=True)

    mean = lax.fori_loop(0, cells // chunk, add_up, jnp.zeros((1, ch), F32)) / cells

    def add_sq(k, acc):
        d = flat[pl.ds(k * chunk, chunk), :].astype(F32) - mean
        return acc + jnp.sum(d * d, axis=0, keepdims=True)

    m2 = lax.fori_loop(0, cells // chunk, add_sq, jnp.zeros((1, ch), F32))
    s1[f, 0:1, :] = mean
    s1[f, 1:2, :] = m2

    pl.semaphore_wait(barrier, (nf - 1) + (nt - 1) + 4)

    def send_frame(buf, ss, rs):
        @pl.loop(1, nf)
        def _(i):
            to = (f + i) % nf
            rcopy(buf.at[f], buf.at[f], ss.at[to], rs.at[f], (to, t)).start()

    def wait_frame(buf, ss, rs):
        @pl.loop(1, nf)
        def _(i):
            to = (f + i) % nf
            rcopy(buf.at[to], buf.at[to], ss.at[to], rs.at[to], (to, t)).wait()

    def send_tile(buf, ss, rs):
        @pl.loop(1, nt)
        def _(i):
            to = (t + i) % nt
            rcopy(buf.at[t], buf.at[t], ss.at[to], rs.at[t], (f, to)).start()

    def wait_tile(buf, ss, rs):
        @pl.loop(1, nt)
        def _(i):
            to = (t + i) % nt
            rcopy(buf.at[to], buf.at[to], ss.at[to], rs.at[to], (f, to)).wait()

    send_frame(s1, s1_s, s1_r)

    halo = [
        rcopy(cot, ext.at[2:4, 1:7], halo_s.at[0], halo_r.at[0], at(-1, 0)),
        rcopy(cot.at[:, 0], ext.at[0:2, 7], halo_s.at[1], halo_r.at[1], at(0, -1)),
        rcopy(cot.at[:, 5], ext.at[0:2, 0], halo_s.at[2], halo_r.at[2], at(0, 1)),
        rcopy(cot.at[:, 0], ext.at[2:4, 7], halo_s.at[3], halo_r.at[3], at(-1, -1)),
        rcopy(cot.at[:, 5], ext.at[2:4, 0], halo_s.at[4], halo_r.at[4], at(-1, 1)),
    ]
    for c in halo:
        c.start()
    ext[0:2, 1:7] = cot[...]

    def combine(buf, each):
        m = buf[:, 0, :]
        n = m.shape[0]
        avg = jnp.sum(m, axis=0, keepdims=True) / n
        d = m - avg
        return avg, jnp.sum(buf[:, 1, :], axis=0, keepdims=True) + each * jnp.sum(
            d * d, axis=0, keepdims=True
        )

    wait_frame(s1, s1_s, s1_r)
    avg, m2 = combine(s1, float(cells))
    s2[t, 0:1, :] = avg
    s2[t, 1:2, :] = m2
    send_tile(s2, s2_s, s2_r)

    for c in halo:
        c.wait()

    @pl.when(t == 0)
    def _():
        ext[:, 0] = jnp.zeros((4, cols, ch), BF16)

    @pl.when(t == nt - 1)
    def _():
        ext[:, 7] = jnp.zeros((4, cols, ch), BF16)

    @pl.when(f == nf - 1)
    def _():
        ext[2:4] = jnp.zeros((2, 8, cols, ch), BF16)

    @pl.loop(0, 4 * 8)
    def _(k):
        p, r = k // 8, k % 8
        v = ext[p, r].astype(F32)
        col = lax.broadcasted_iota(jnp.int32, v.shape, 0)
        up = jnp.where(col == cols - 1, 0.0, pltpu.roll(v, cols - 1, 0))
        down = jnp.where(col == 0, 0.0, pltpu.roll(v, 1, 0))
        cotx[p, r, :, 0:ch] = up.astype(BF16)
        cotx[p, r, :, ch : 2 * ch] = ext[p, r]
        cotx[p, r, :, 2 * ch : 3 * ch] = down.astype(BF16)

    def patch(k):
        a, b = k // 3, k % 3
        return cotx[pl.ds(2 - a, frames), pl.ds(2 - b, rows)].reshape(cells, 3 * ch)

    gact[...] = jnp.zeros_like(gact)

    @pl.loop(0, 9)
    def _(k):
        taps = jnp.concatenate([w[3 * k], w[3 * k + 1], w[3 * k + 2]], axis=1)
        gact[...] += lax.dot_general(
            patch(k), taps, (((1,), (1,)), ((), ())), preferred_element_type=F32
        )

    wait_tile(s2, s2_s, s2_r)
    avg, m2 = combine(s2, float(cells * nf))
    per_channel = float(cells * nf * nt)
    group = ch // GROUPS
    g_avg = group_sum(avg) / group
    d = avg - g_avg
    spread = group_sum(m2 + per_channel * (d * d)) / (per_channel * group)
    inv = lax.rsqrt(spread + EPS)

    gw, bw = gain[...], bias[...]

    def norm(k, acc):
        at_rows = pl.ds(k * chunk, chunk)
        xh = (flat[at_rows, :].astype(F32) - g_avg) * inv
        nrm = xh * gw + bw
        s = 1.0 / (1.0 + jnp.exp(-nrm))
        act = (nrm * s).astype(BF16).astype(F32)
        act_t[:, at_rows] = act.T.astype(BF16)
        gn = gact[at_rows, :] * s * (1.0 + nrm * (1.0 - s))
        gact[at_rows, :] = gn
        xhat[at_rows, :] = xh
        return (
            acc[0] + jnp.sum(gn * xh, axis=0, keepdims=True),
            acc[1] + jnp.sum(gn, axis=0, keepdims=True),
        )

    zero = jnp.zeros((1, ch), F32)
    sums = (zero, zero)
    for k in range(cells // chunk):
        sums = norm(k, sums)
    g1[f, 0:1, :] = sums[0]
    g1[f, 1:2, :] = sums[1]
    send_frame(g1, g1_s, g1_r)

    part[:, :, :, 27] = jnp.zeros((2, 2, NX, 8, ch), F32)

    @pl.loop(0, 9)
    def _(k):
        got = jnp.dot(act_t[...], patch(k), preferred_element_type=F32)
        for e in range(3):
            part[:, :, :, 3 * k + e] = got[:, e * ch : (e + 1) * ch].reshape(2, 2, NX, 8, ch)

    other = 1 - core
    swap = rcopy(part.at[other], rc, core_s.at[0], core_r.at[0], (f, z * 2 + other))
    swap.start()

    wait_frame(g1, g1_s, g1_r)
    g2[t, 0:1, :] = jnp.sum(g1[:, 0, :], axis=0, keepdims=True)
    g2[t, 1:2, :] = jnp.sum(g1[:, 1, :], axis=0, keepdims=True)
    send_tile(g2, g2_s, g2_r)

    swap.wait()
    mine = part.at[core]

    @pl.loop(0, 2)
    def _(h):
        @pl.loop(0, NX)
        def _(i):
            mine[h, i] += rc[h, i]

    first = []
    for i in range(1, 4):
        xo, yo = (x + i) % NX, (y + i) % NY
        first.append(rcopy(mine.at[0, xo], ra1.at[i - 1], st_s.at[0, i], st_r.at[0, i], (y * NX + xo, t)))
        first.append(
            rcopy(mine.at[1, :, pl.ds(yo * TY, TY)], rb1.at[i - 1], st_s.at[1, i], st_r.at[1, i], (yo * NX + x, t))
        )
    for c in first:
        c.start()
    for c in first:
        c.wait()
    mine[0, x] += ra1[0] + ra1[1] + ra1[2]
    own_y = pl.ds(y * TY, TY)
    mine[1, :, own_y] += rb1[0] + rb1[1] + rb1[2]

    second = []
    for i in range(1, 4):
        xo, yo = (x + i) % NX, (y + i) % NY
        second.append(
            rcopy(mine.at[0, x, pl.ds(yo * TY, TY)], ra2.at[i - 1], st_s.at[2, i], st_r.at[2, i], (yo * NX + x, t))
        )
        second.append(
            rcopy(mine.at[1, xo, own_y], rb2.at[i - 1], st_s.at[3, i], st_r.at[3, i], (y * NX + xo, t))
        )
    for c in second:
        c.start()
    for c in second:
        c.wait()
    zsrc[0:TY] = mine[0, x, own_y] + (ra2[0] + ra2[1] + ra2[2])
    zsrc[TY:NTILES] = mine[1, x, own_y] + (rb2[0] + rb2[1] + rb2[2])

    def zdev(j):
        return (f, j * 2 + core)

    @pl.loop(0, NTILES)
    def _(j):
        @pl.when(j != z)
        def _():
            rcopy(zsrc.at[j], rz.at[z], z_s.at[j], z_r.at[z], zdev(j)).start()

    wait_tile(g2, g2_s, g2_r)
    d_gain = jnp.sum(g2[:, 0, :], axis=0, keepdims=True)
    d_shift = jnp.sum(g2[:, 1, :], axis=0, keepdims=True)
    gs[0:1, :] = d_gain
    gs[1:2, :] = d_shift
    count = per_channel * group
    g_mean = group_sum(gw * d_shift) / count
    g_proj = group_sum(gw * d_gain) / count

    out = fg.reshape(cells, ch)

    @pl.loop(0, cells // chunk)
    def _(k):
        at_rows = pl.ds(pl.multiple_of(k * chunk, chunk), chunk)
        out[at_rows, :] = (
            inv * (gact[at_rows, :] * gw - g_mean - xhat[at_rows, :] * g_proj)
        ).astype(BF16)

    @pl.loop(0, NTILES)
    def _(j):
        @pl.when(j != z)
        def _():
            rcopy(zsrc.at[j], rz.at[z], z_s.at[j], z_r.at[z], zdev(j)).wait_send()

    @pl.when(z < NTILES)
    def _():
        rz[z] = zsrc[z]

        @pl.loop(1, NZ)
        def _(i):
            j = (z + i) % NZ
            rcopy(zsrc.at[0], rz.at[j], z_s.at[0], z_r.at[j], zdev(j)).wait_recv()

        zg[z] = jnp.sum(rz[...], axis=0)

        @pl.loop(1, NZ)
        def _(i):
            j = (z + i) % NZ
            rcopy(zg.at[z], zg.at[z], zg_s.at[j], zg_r.at[z], zdev(j)).start()

        @pl.loop(1, NZ)
        def _(i):
            j = (z + i) % NZ
            rcopy(zg.at[z], zg.at[z], zg_s.at[j], zg_r.at[z], zdev(j)).wait_send()

    @pl.loop(0, NTILES)
    def _(j):
        @pl.when(j != z)
        def _():
            rcopy(zg.at[j], zg.at[j], zg_s.at[0], zg_r.at[j], zdev(j)).wait_recv()

    full = gk.at[core]
    full[0, x, own_y] = zg[0:TY]
    full[1, x, own_y] = zg[TY:NTILES]

    def spread_out(half_x, stage):
        sends, arrivals = [], []
        for i in range(1, 4):
            xo, yo = (x + i) % NX, (y + i) % NY
            for half, axis_x in ((half_x, True), (1 - half_x, False)):
                dev = (y * NX + xo, t) if axis_x else (yo * NX + x, t)
                xa, ya = (xo, y) if axis_x else (x, yo)
                if stage == 0:
                    here = full.at[half, x, own_y]
                    there = full.at[half, xa, pl.ds(ya * TY, TY)]
                elif axis_x:
                    here = full.at[half, x]
                    there = full.at[half, xo]
                else:
                    here = full.at[half, :, own_y]
                    there = full.at[half, :, pl.ds(yo * TY, TY)]
                k = 2 * stage + half
                mine_at = x if axis_x else y
                from_at = xo if axis_x else yo
                sends.append(rcopy(here, here, ag_s.at[k, from_at], ag_r.at[k, mine_at], dev))
                arrivals.append(rcopy(there, there, ag_s.at[k, from_at], ag_r.at[k, from_at], dev))
        for c in sends:
            c.start()
        for c in sends:
            c.wait_send()
        for c in arrivals:
            c.wait_recv()

    spread_out(1, 0)
    spread_out(0, 1)

    last = rcopy(full, full, core_s.at[1], core_r.at[1], (f, z * 2 + other))
    last.start()
    last.wait_send()
    rcopy(gk.at[other], gk.at[other], core_s.at[1], core_r.at[1], (f, z * 2 + other)).wait_recv()


def on_device(features, norm_gain_weight, norm_bias, kernel, cotangent):
    frames, rows, cols, ch = features.shape
    cells = frames * rows * cols
    nf, nt = NX * NY, NZ * 2
    vm = pl.BlockSpec(memory_space=pltpu.VMEM)
    dma = pltpu.SemaphoreType.DMA
    fg, gk, gs = pl.pallas_call(
        body,
        out_shape=(
            jax.ShapeDtypeStruct(features.shape, BF16),
            jax.ShapeDtypeStruct((2, 2, NX, TAPS, 8, ch), F32),
            jax.ShapeDtypeStruct((2, ch), F32),
        ),
        in_specs=[vm] * 5,
        out_specs=(vm, vm, vm),
        scratch_shapes=[
            pltpu.VMEM((4, rows + 2, cols, ch), BF16),
            pltpu.VMEM((4, rows + 2, cols, 3 * ch), BF16),
            pltpu.VMEM((cells, ch), F32),
            pltpu.VMEM((cells, ch), F32),
            pltpu.VMEM((ch, cells), BF16),
            pltpu.VMEM((nf, 2, ch), F32),
            pltpu.VMEM((nt, 2, ch), F32),
            pltpu.VMEM((nf, 2, ch), F32),
            pltpu.VMEM((nt, 2, ch), F32),
            pltpu.VMEM((2, 2, NX, TAPS, 8, ch), F32),
            pltpu.VMEM((2, NX, TAPS, 8, ch), F32),
            pltpu.VMEM((3, TAPS, 8, ch), F32),
            pltpu.VMEM((3, NX, TY, 8, ch), F32),
            pltpu.VMEM((3, TY, 8, ch), F32),
            pltpu.VMEM((3, TY, 8, ch), F32),
            pltpu.VMEM((NTILES, 8, ch), F32),
            pltpu.VMEM((NZ, 8, ch), F32),
            pltpu.VMEM((NTILES, 8, ch), F32),
            dma((5,)), dma((5,)),
            dma((nf,)), dma((nf,)), dma((nt,)), dma((nt,)),
            dma((nf,)), dma((nf,)), dma((nt,)), dma((nt,)),
            dma((2,)), dma((2,)),
            dma((4, 4)), dma((4, 4)),
            dma((NZ,)), dma((NZ,)), dma((NZ,)), dma((NZ,)),
            dma((4, 4)), dma((4, 4)),
        ],
        compiler_params=pltpu.CompilerParams(
            collective_id=0, has_side_effects=True, vmem_limit_bytes=40 * 2**20
        ),
    )(
        features,
        norm_gain_weight.reshape(1, ch),
        norm_bias.reshape(1, ch),
        kernel.reshape(27, ch, ch),
        cotangent,
    )
    grad_kernel = jnp.transpose(gk, (3, 0, 1, 2, 4, 5))[:27].reshape(3, 3, 3, ch, ch)
    return fg, grad_kernel, gs[0], gs[1]


def solution(mesh):
    placed = (P("frame", "tile", None, None), P(), P(), P(), P("frame", "tile", None, None))
    return jax.shard_map(
        on_device,
        mesh=mesh,
        in_specs=placed,
        out_specs=(P("frame", "tile", None, None), P(), P(), P()),
        check_vma=False,
    )
```

time: 863 us -> 86.8 us (0.10)
  waiting for transfers between devices: 473 us -> 0 us
  blocking collectives: 311 us -> 0 us
  Pallas kernels: 0 us -> 78.9 us
  local copies, waits for them, and re-layouts: 25.6 us -> 7.09 us
  starting transfers between devices: 18 us -> 0 us
  between operations: 14.7 us -> 0.66 us
  other arithmetic: 13.6 us -> 0 us
    psum x1 -> x0, waiting for transfers between devices: 466 us -> none  [on_device(): grad_kernel = lax.psum(local_kernel, ('frame', 'tile'))]
    psum x3 -> x0, blocking collectives: 311 us -> none  [the longest x1 109 us: on_device(): lax.psum(jnp.sum(grouped, axis=(0, 2)), ('frame', 'tile')) / cell_count]
    pallas_call x0 -> x1, Pallas kernels: none -> 78.9 us  [on_device(): pl.pallas_call(body, out_shape=(jax.ShapeDtypeStruct(features.shape, BF16...]
    ppermute x6 -> x0, starting transfers between devices: 17.9 us -> none  [the longest x2 8.51 us: padded(): lax.ppermute(tail, axis, [(i, (i + 1) % count) for i in range(ends)])]
    reshape x11 -> x0, local copies, waits for them, and re-layouts: 11 us -> none  [the longest x9 10.9 us: on_device(): patches = jnp.concatenate([act_full[frame_tap:frame_tap + frames, row_tap...]
    concatenate x15 -> x0, other arithmetic: 9.16 us -> none  [the longest x7 8.14 us: on_device(): jnp.concatenate([act_full[frame_tap:frame_tap + frames, row_tap:row_tap +...]
  transfers between devices with their start and end apart: 7 -> 0, of which waited for: 3 -> 0; matrix products, arithmetic and copies ran while one was open for 1% -> 0% of each run, Pallas kernels for 0% -> 0%
where the time goes in v1:
time: 86.8 us; the launch traced here: 86.6 us
  Pallas kernels  78.9 us (91%)
  local copies, waits for them, and re-layouts  7.09 us (8%)
    pallas_call x1, Pallas kernels, on_device(): pl.pallas_call(body, out_shape=(jax.ShapeDtypeStruct(features.shape, BF16...  78.9 us
    unnamed x11, local copies, waits for them, and re-layouts  5 us

profile of v1, /device:TPU:1, one launch (start us, length us, event | category | flops | bytes accessed | tf_op | source)
XLA Modules:
  0.0 86.6 jit_solution(8941468522466714909)
XLA Ops:
  0.6 0.0 copy-start
  0.6 1.2 %copy-done = bf16[3,3,3,128,128]{4,3,2,1,0:T(8,128)(2,1)S(1)} copy-done((bf16[3,3,3,128,128]{4,3,2,1,0:T(8,128)(2,1)S(1)}, bf16[3,3,3,128,128]{4,3,2,1,0:T(8,128)(2,1)}, u32[]{:S(2)}) %copy-start) | copy-done | bytes 884760
  1.8 0.0 copy-start.1
  1.8 0.9 %copy-done.1 = bf16[2,6,64,128]{3,2,1,0:T(8,128)(2,1)S(1)} copy-done((bf16[2,6,64,128]{3,2,1,0:T(8,128)(2,1)S(1)}, bf16[2,6,64,128]{3,2,1,0:T(8,128)(2,1)}, u32[]{:S(2)}) %copy-start.1) | copy-done | bytes 196632
  2.7 0.0 copy-start.2
  2.7 0.9 %copy-done.2 = bf16[2,6,64,128]{3,2,1,0:T(8,128)(2,1)S(1)} copy-done((bf16[2,6,64,128]{3,2,1,0:T(8,128)(2,1)S(1)}, bf16[2,6,64,128]{3,2,1,0:T(8,128)(2,1)}, u32[]{:S(2)}) %copy-start.2) | copy-done | bytes 196632
  3.7 0.0 copy-start.3
  3.7 0.7 copy-done.3
  4.3 0.0 copy-start.4
  4.3 0.7 copy-done.4
  5.0 78.9 %shard_map.84 = (bf16[2,6,64,128]{3,2,1,0:T(8,128)(2,1)S(1)}, f32[2,2,4,28,8,128]{5,4,3,2,1,0:T(8,128)S(1)}, f32[2,128]{1,0:T(2,128)S(1)}) custom-call(bf16[2,6,64,128]{3,2,1,0:T(8,128)(2,1)S(1)} %copy-done.1, f32[1,128]{1,0:T(1,128)S(1)} %bitcast.11, f32[1,128]{1,0:T(1,128)S(1)} %bitcast.12, bf16[27,128,128]{2,1,0:T(8,128)(2,1)S(1)} %bitcast.10, ...), custom_call_target="tpu_custom_call" | custom-call | tf_op jit(solution)/shard_map/pallas_call | solution.py:379
  83.8 0.1 slice.12
  84.0 1.5 %copy.9 = f32[27,2,2,4,8,128]{5,4,3,2,1,0:T(8,128)} copy(f32[27,2,2,4,8,128]{5,4,0,3,2,1:T(8,128)S(1)} %slice.12) | data formatting | bytes 3538944 | tf_op jit(solution)/shard_map/slice | solution.py:425
  85.4 0.5 slice_bitcast_fusion
  85.9 0.7 copy.11
Async XLA Ops:
  0.6 1.2 %copy-start = (bf16[3,3,3,128,128]{4,3,2,1,0:T(8,128)(2,1)S(1)}, bf16[3,3,3,128,128]{4,3,2,1,0:T(8,128)(2,1)}, u32[]{:S(2)}) copy-start(bf16[3,3,3,128,128]{4,3,2,1,0:T(8,128)(2,1)} %param.8) | copy-start | bytes 2654212
  1.8 0.9 %copy-start.1 = (bf16[2,6,64,128]{3,2,1,0:T(8,128)(2,1)S(1)}, bf16[2,6,64,128]{3,2,1,0:T(8,128)(2,1)}, u32[]{:S(2)}) copy-start(bf16[2,6,64,128]{3,2,1,0:T(8,128)(2,1)} %feat.1) | copy-start | bytes 589828
  2.7 0.9 %copy-start.2 = (bf16[2,6,64,128]{3,2,1,0:T(8,128)(2,1)S(1)}, bf16[2,6,64,128]{3,2,1,0:T(8,128)(2,1)}, u32[]{:S(2)}) copy-start(bf16[2,6,64,128]{3,2,1,0:T(8,128)(2,1)} %cot.1) | copy-start | bytes 589828
  3.7 0.7 copy-start.3
  4.3 0.7 copy-start.4

commit v2 on v0

v2 whole, which is shorter than its diff:
```python
import functools

import jax
import jax.numpy as jnp
from jax import lax
from jax.experimental import pallas as pl
from jax.experimental.pallas import tpu as pltpu
from jax.sharding import PartitionSpec as P

MESH = pl.DeviceIdType.MESH
GROUPS = 32
EPS = 1e-06
NX = 4
NY = 4
NZ = 16
NF = NX * NY
LAST = 26
HALF = 7
F32 = jnp.float32
BF16 = jnp.bfloat16
CHUNK = 128


def group_sum(v):
    lane = lax.broadcasted_iota(jnp.int32, v.shape, 1)
    v = v + jnp.where(lane % 2 == 0, pltpu.roll(v, 127, 1), pltpu.roll(v, 1, 1))
    return v + jnp.where(lane % 4 < 2, pltpu.roll(v, 126, 1), pltpu.roll(v, 2, 1))


def rcopy(src, dst, ss, rs, dev):
    return pltpu.make_async_remote_copy(
        src_ref=src, dst_ref=dst, send_sem=ss, recv_sem=rs, device_id=dev, device_id_type=MESH
    )


def body(
    stop,
    feat_h, gain_h, bias_h, w_h, cot_h,
    fg, gk, gs,
    fx, gain, bias, w, ext, cotx, gact, xhat, act_t,
    s0, s1, s2, g0, g1, g2,
    part, ra1, rb1, ra2, rb2, zsrc, rz,
    load_s, halo_s, halo_r, sm_s, sm_r, st_s, st_r, z_s, z_r, ag_s, ag_r, fw_s, fw_r,
):
    f, t = lax.axis_index("frame"), lax.axis_index("tile")
    y, x = f // NX, lax.rem(f, NX)
    z, core = t // 2, lax.rem(t, 2)
    other = 1 - core
    _, frames, rows, cols, ch = fx.shape
    cells = frames * rows * cols
    mate = (f, z * 2 + other)
    zn = lax.rem(z - 1 + 2 * core + NZ, NZ)
    fdevs = [(lax.rem(f + i, NF), t) for i in range(1, NF)]
    far = sorted(range(1, NZ), key=lambda i: -min(i, NZ - i))
    zs = [lax.rem(z + i, NZ) for i in far]
    zdevs = [(f, j * 2 + core) for j in zs]
    xs = [lax.rem(x + i, NX) for i in range(1, NX)]
    ys = [lax.rem(y + i, NY) for i in range(1, NY)]
    xdevs = [(y * NX + i, t) for i in xs]
    ydevs = [(i * NX + x, t) for i in ys]
    own_rows = pl.ds(1 + rows * core, rows)
    mate_rows = pl.ds(1 + rows * other, rows)

    loads = [
        pltpu.make_async_copy(feat_h, fx.at[core], load_s.at[0]),
        pltpu.make_async_copy(cot_h, ext.at[0:2, own_rows], load_s.at[1]),
        pltpu.make_async_copy(w_h, w, load_s.at[2]),
        pltpu.make_async_copy(gain_h, gain, load_s.at[3]),
        pltpu.make_async_copy(bias_h, bias, load_s.at[4]),
    ]
    for c in loads:
        c.start()

    barrier = pltpu.get_barrier_semaphore()
    greet = zdevs + fdevs + [mate, (f, zn * 2 + other)]
    for dev in greet:
        pl.semaphore_signal(barrier, inc=1, device_id=dev, device_id_type=MESH)

    loads[0].wait()
    flat = fx.reshape(2, cells, ch)
    chunks = cells // CHUNK

    def add_up(k, acc):
        return acc + jnp.sum(flat[core, pl.ds(k * CHUNK, CHUNK), :].astype(F32), axis=0, keepdims=True)

    mean = lax.fori_loop(0, chunks, add_up, jnp.zeros((1, ch), F32)) / cells

    def add_sq(k, acc):
        d = flat[core, pl.ds(k * CHUNK, CHUNK), :].astype(F32) - mean
        return acc + jnp.sum(d * d, axis=0, keepdims=True)

    m2 = lax.fori_loop(0, chunks, add_sq, jnp.zeros((1, ch), F32))
    s0[core, 0:1, :] = mean
    s0[core, 1:2, :] = m2
    loads[1].wait()

    pl.semaphore_wait(barrier, len(greet))
    if stop == 1:
        for c in loads[2:]:
            c.wait()
        return

    def fan(buf, me, devs, k):
        for dev in devs:
            rcopy(buf.at[me], buf.at[me], sm_s.at[k], sm_r.at[k], dev).start()

    def fan_recv(buf, k, n):
        many = buf.at[pl.ds(0, n)]
        rcopy(many, many, sm_s.at[k], sm_r.at[k], mate).wait_recv()

    def fan_sent(buf, k, n):
        many = buf.at[pl.ds(0, n)]
        rcopy(many, many, sm_s.at[k], sm_r.at[k], mate).wait_send()

    fan(s0, core, [mate], 0)
    block = ext.at[0:2, own_rows]
    to_mate = rcopy(block, block, halo_s.at[0], halo_r.at[0], mate)
    feats = rcopy(fx.at[core], fx.at[core], halo_s.at[1], halo_r.at[1], mate)
    edge_src, edge_dst = ext.at[0:2, 1 + (2 * rows - 1) * core], ext.at[0:2, (2 * rows + 1) * other]
    edges = [
        rcopy(edge_src, edge_dst, halo_s.at[2 + c], halo_r.at[2 + core], (f, zn * 2 + c)) for c in range(2)
    ]
    edge_in = [
        rcopy(ext.at[0:2, 2 * rows + 1], ext.at[0:2, 2 * rows + 1], halo_s.at[2], halo_r.at[2], mate),
        rcopy(ext.at[0:2, 0], ext.at[0:2, 0], halo_s.at[3], halo_r.at[3], mate),
    ]
    for c in [feats, to_mate] + edges:
        c.start()

    def combine(buf, each):
        m = buf[:, 0, :]
        n = m.shape[0]
        avg = jnp.sum(m, axis=0, keepdims=True) / n
        d = m - avg
        return avg, jnp.sum(buf[:, 1, :], axis=0, keepdims=True) + each * jnp.sum(
            d * d, axis=0, keepdims=True
        )

    fan_recv(s0, 0, 1)
    avg, m2 = combine(s0, float(cells))
    s1[f, 0:1, :] = avg
    s1[f, 1:2, :] = m2
    fan(s1, f, fdevs, 1)

    before = (lax.rem(f - 1 + NF, NF), t)
    later = ext.at[2:4, own_rows]
    to_before = rcopy(block, later, halo_s.at[4], halo_r.at[4], before)
    to_before.start()

    for c in edge_in:
        c.wait_recv()

    @pl.when(z == 0)
    def _():
        ext[0:2, 0] = jnp.zeros((2, cols, ch), BF16)

    @pl.when(z == NZ - 1)
    def _():
        ext[0:2, 2 * rows + 1] = jnp.zeros((2, cols, ch), BF16)

    rims = [
        rcopy(ext.at[0:2, r], ext.at[2:4, r], halo_s.at[k], halo_r.at[k], before)
        for k, r in ((5, 0), (6, 2 * rows + 1))
    ]
    for c in rims:
        c.start()

    fan_recv(s1, 1, NF - 1)
    avg, m2 = combine(s1, float(cells * 2))
    s2[z, 0:1, :] = avg
    s2[z, 1:2, :] = m2
    fan(s2, z, zdevs, 2)

    to_before.wait_recv()
    relay = rcopy(later, later, halo_s.at[7], halo_r.at[7], mate)
    relay.start()
    to_mate.wait()
    feats.wait()
    for c in edges:
        c.wait_send()
    to_before.wait_send()
    for c in rims:
        c.wait()
    relay.wait()
    fan_sent(s0, 0, 1)
    fan_sent(s1, 1, NF - 1)

    @pl.when(f == NF - 1)
    def _():
        ext[2:4] = jnp.zeros((2, 2 * rows + 2, cols, ch), BF16)

    @pl.loop(0, 4 * (2 * rows + 2))
    def _(k):
        p, r = k // (2 * rows + 2), lax.rem(k, 2 * rows + 2)
        v = ext[p, r].astype(F32)
        col = lax.broadcasted_iota(jnp.int32, v.shape, 0)
        up = jnp.where(col == cols - 1, 0.0, pltpu.roll(v, cols - 1, 0))
        down = jnp.where(col == 0, 0.0, pltpu.roll(v, 1, 0))
        cotx[0, p, r] = up.astype(BF16)
        cotx[1, p, r] = ext[p, r]
        cotx[2, p, r] = down.astype(BF16)

    for c in loads[2:]:
        c.wait()
    gact[...] = jnp.zeros_like(gact)

    @pl.loop(0, 9)
    def _(k):
        a, b = k // 3, lax.rem(k, 3)
        p, r = pl.ds(2 - a, frames), pl.ds(2 - b + rows * core, rows)
        taps = jnp.concatenate([w[3 * k], w[3 * k + 1], w[3 * k + 2]], axis=1)
        patch = jnp.concatenate([cotx[e, p, r].reshape(cells, ch) for e in range(3)], axis=1)
        gact[...] += lax.dot_general(patch, taps, (((1,), (1,)), ((), ())), preferred_element_type=F32)

    fan_recv(s2, 2, NZ - 1)
    fan_sent(s2, 2, NZ - 1)
    if stop == 2:
        return
    avg, m2 = combine(s2, float(cells * 2 * NF))
    per_channel = float(cells * 2 * NF * NZ)
    group = ch // GROUPS
    g_avg = group_sum(avg) / group
    d = avg - g_avg
    spread = group_sum(m2 + per_channel * (d * d)) / (per_channel * group)
    inv = lax.rsqrt(spread + EPS)
    gw, bw = gain[...], bias[...]

    def normed(c, k):
        xh = (flat[c, pl.ds(k * CHUNK, CHUNK), :].astype(F32) - g_avg) * inv
        nrm = xh * gw + bw
        return xh, nrm, 1.0 / (1.0 + jnp.exp(-nrm))

    @pl.loop(0, 2 * chunks)
    def _(k):
        c, kk = k // chunks, lax.rem(k, chunks)
        _, nrm, s = normed(c, kk)
        act = (nrm * s).astype(BF16)
        per = chunks // frames
        to = (kk // per) * (2 * per) + c * per + lax.rem(kk, per)
        act_t[to] = act.T

    def pair(q):
        got = []
        for n in range(2):
            tap = jnp.minimum(core * (2 * HALF) + 2 * q + n, LAST)
            a, b, e = tap // 9, lax.rem(tap // 3, 3), lax.rem(tap, 3)
            got.append(
                cotx[e, pl.ds(2 - a, frames), pl.ds(2 - b, 2 * rows)].reshape(2 * cells, ch)
            )
        acts = jnp.concatenate([act_t[i] for i in range(2 * chunks)], axis=1)
        out = jnp.dot(acts, jnp.concatenate(got, axis=1), preferred_element_type=F32)
        for n in range(2):
            j = 2 * q + n
            part[j // HALF, :, :, lax.rem(j, HALF)] = out[:, n * ch : (n + 1) * ch].reshape(NX, NY, 8, ch)

    pl.loop(0, 4)(pair)
    a1 = [
        rcopy(part.at[0, xo], ra1.at[i], st_s.at[0, i], st_r.at[0, i], dev)
        for i, (xo, dev) in enumerate(zip(xs, xdevs))
    ]
    for c in a1:
        c.start()
    pl.loop(4, HALF)(pair)
    b1 = [
        rcopy(part.at[1, :, yo], rb1.at[i], st_s.at[1, i], st_r.at[1, i], dev)
        for i, (yo, dev) in enumerate(zip(ys, ydevs))
    ]
    for c in b1:
        c.start()

    def norm_grad(k, acc):
        at_rows = pl.ds(k * CHUNK, CHUNK)
        xh, nrm, s = normed(core, k)
        gn = gact[at_rows, :] * s * (1.0 + nrm * (1.0 - s))
        gact[at_rows, :] = gn
        xhat[at_rows, :] = xh
        return (
            acc[0] + jnp.sum(gn * xh, axis=0, keepdims=True),
            acc[1] + jnp.sum(gn, axis=0, keepdims=True),
        )

    zero = jnp.zeros((1, ch), F32)
    d_gain, d_shift = lax.fori_loop(0, chunks, norm_grad, (zero, zero))
    g0[core, 0:1, :] = d_gain
    g0[core, 1:2, :] = d_shift
    fan(g0, core, [mate], 3)

    def pass_on(buf, k, n, to, me, devs):
        fan_recv(buf, k, n)
        to[me, 0:1, :] = jnp.sum(buf[:, 0, :], axis=0, keepdims=True)
        to[me, 1:2, :] = jnp.sum(buf[:, 1, :], axis=0, keepdims=True)
        fan(to, me, devs, k + 1)
        fan_sent(buf, k, n)

    pass_on(g0, 3, 1, g1, f, fdevs)

    for c in a1:
        c.wait_recv()
    part[0, x] += ra1[0] + ra1[1] + ra1[2]
    a2 = [
        rcopy(part.at[0, x, yo], ra2.at[i], st_s.at[2, i], st_r.at[2, i], dev)
        for i, (yo, dev) in enumerate(zip(ys, ydevs))
    ]
    for c in a2:
        c.start()
    for c in b1:
        c.wait_recv()
    part[1, :, y] += rb1[0] + rb1[1] + rb1[2]
    b2 = [
        rcopy(part.at[1, xo, y], rb2.at[i], st_s.at[3, i], st_r.at[3, i], dev)
        for i, (xo, dev) in enumerate(zip(xs, xdevs))
    ]
    for c in b2:
        c.start()

    pass_on(g1, 4, NF - 1, g2, z, zdevs)

    def z_send(h):
        for j in range(HALF):
            q = 2 * j + h

            @pl.when(z != q)
            def _():
                rcopy(zsrc.at[h, j], rz.at[z], z_s.at[0, q], z_r.at[0], (f, q * 2 + core)).start()

    for c in a2:
        c.wait_recv()
    zsrc[0] = part[0, x, y] + (ra2[0] + ra2[1] + ra2[2])
    z_send(0)
    for c in b2:
        c.wait_recv()
    zsrc[1] = part[1, x, y] + (rb2[0] + rb2[1] + rb2[2])
    z_send(1)
    for c in a1 + b1 + a2 + b2:
        c.wait_send()

    full = gk.at[core]
    mine = full.at[:, x, y]

    @pl.when(z < 2 * HALF)
    def _():
        h, j = lax.rem(z, 2), z // 2
        rz[z] = zsrc[h, j]
        many = rz.at[pl.ds(0, NZ - 1)]
        rcopy(many, many, z_s.at[0, 0], z_r.at[0], mate).wait_recv()
        mine[h, j] = jnp.sum(rz[...], axis=0)
        for jz, dev in zip(zs, zdevs):
            rcopy(mine.at[h, j], mine.at[h, j], z_s.at[1, jz], z_r.at[1 + z], dev).start()

    fan_recv(g2, 5, NZ - 1)
    fan_sent(g2, 5, NZ - 1)
    d_gain = jnp.sum(g2[:, 0, :], axis=0, keepdims=True)
    d_shift = jnp.sum(g2[:, 1, :], axis=0, keepdims=True)
    gs[0:1, :] = d_gain
    gs[1:2, :] = d_shift
    count = per_channel * group
    g_mean = group_sum(gw * d_shift) / count
    g_proj = group_sum(gw * d_gain) / count
    out = fg.reshape(cells, ch)

    @pl.loop(0, chunks)
    def _(k):
        at_rows = pl.ds(pl.multiple_of(k * CHUNK, CHUNK), CHUNK)
        out[at_rows, :] = (
            inv * (gact[at_rows, :] * gw - g_mean - xhat[at_rows, :] * g_proj)
        ).astype(BF16)

    for h in range(2):
        for j in range(HALF):
            q = 2 * j + h

            @pl.when(z != q)
            def _():
                rcopy(zsrc.at[h, j], rz.at[z], z_s.at[0, q], z_r.at[0], (f, q * 2 + core)).wait_send()

    def z_recv(h):
        for j in range(HALF):
            q = 2 * j + h

            @pl.when(z != q)
            def _():
                rcopy(mine.at[h, j], mine.at[h, j], z_s.at[1, 0], z_r.at[1 + q], mate).wait_recv()

    def gather(here, there, k, devs):
        sends = [rcopy(here, here, ag_s.at[k, i], ag_r.at[k, i], dev) for i, dev in enumerate(devs)]
        come = [rcopy(p, p, ag_s.at[k, i], ag_r.at[k, i], mate) for i, p in enumerate(there)]
        for c in sends:
            c.start()
        return sends, come

    def behind(v, n):
        return [lax.rem(v - i + n, n) for i in range(1, n)]

    xb, yb = behind(x, NX), behind(y, NY)

    def forward(piece, h, i):
        c = rcopy(piece, piece, fw_s.at[h, i], fw_r.at[h, i], mate)
        c.start()
        return c

    z_recv(0)
    a_out, a_in = gather(full.at[0, x, y], [full.at[0, x, i] for i in yb], 0, ydevs)
    z_recv(1)
    b_out, b_in = gather(full.at[1, x, y], [full.at[1, i, y] for i in xb], 1, xdevs)
    for c in a_in:
        c.wait_recv()
    a_out2, a_in2 = gather(full.at[0, x], [full.at[0, i] for i in xb], 2, xdevs)
    fw = [forward(full.at[0, x], 0, 0)]
    for c in b_in:
        c.wait_recv()
    b_out2, b_in2 = gather(full.at[1, :, y], [full.at[1, :, i] for i in yb], 3, ydevs)
    fw.append(forward(full.at[1, :, y], 1, 0))
    for i in range(NX - 1):
        a_in2[i].wait_recv()
        fw.append(forward(full.at[0, xb[i]], 0, i + 1))
        b_in2[i].wait_recv()
        fw.append(forward(full.at[1, :, yb[i]], 1, i + 1))

    @pl.when(z < 2 * HALF)
    def _():
        h, j = lax.rem(z, 2), z // 2
        for jz, dev in zip(zs, zdevs):
            rcopy(mine.at[h, j], mine.at[h, j], z_s.at[1, jz], z_r.at[1 + z], dev).wait_send()

    for c in a_out + b_out + a_out2 + b_out2:
        c.wait_send()
    for c in fw:
        c.wait()


def call(stop, cid, features, norm_gain_weight, norm_bias, kernel, cotangent):
    frames, rows, cols, ch = features.shape
    cells = frames * rows * cols
    vm = pl.BlockSpec(memory_space=pltpu.VMEM)
    hbm = pl.BlockSpec(memory_space=pltpu.HBM)
    dma = pltpu.SemaphoreType.DMA
    tile = (8, ch)
    return pl.pallas_call(
        functools.partial(body, stop),
        out_shape=(
            jax.ShapeDtypeStruct(features.shape, BF16),
            jax.ShapeDtypeStruct((2, 2, NX, NY, HALF) + tile, F32),
            jax.ShapeDtypeStruct((2, ch), F32),
        ),
        in_specs=[hbm] * 5,
        out_specs=(vm, vm, vm),
        scratch_shapes=[
            pltpu.VMEM((2,) + features.shape, BF16),
            pltpu.VMEM((1, ch), F32),
            pltpu.VMEM((1, ch), F32),
            pltpu.VMEM((27, ch, ch), BF16),
            pltpu.VMEM((4, 2 * rows + 2, cols, ch), BF16),
            pltpu.VMEM((3, 4, 2 * rows + 2, cols, ch), BF16),
            pltpu.VMEM((cells, ch), F32),
            pltpu.VMEM((cells, ch), F32),
            pltpu.VMEM((2 * cells // CHUNK, ch, CHUNK), BF16),
            pltpu.VMEM((2, 2, ch), F32),
            pltpu.VMEM((NF, 2, ch), F32),
            pltpu.VMEM((NZ, 2, ch), F32),
            pltpu.VMEM((2, 2, ch), F32),
            pltpu.VMEM((NF, 2, ch), F32),
            pltpu.VMEM((NZ, 2, ch), F32),
            pltpu.VMEM((2, NX, NY, HALF) + tile, F32),
            pltpu.VMEM((3, NY, HALF) + tile, F32),
            pltpu.VMEM((3, NX, HALF) + tile, F32),
            pltpu.VMEM((3, HALF) + tile, F32),
            pltpu.VMEM((3, HALF) + tile, F32),
            pltpu.VMEM((2, HALF) + tile, F32),
            pltpu.VMEM((NZ,) + tile, F32),
            dma((5,)), dma((8,)), dma((8,)),
            dma((6,)), dma((6,)),
            dma((4, 3)), dma((4, 3)),
            dma((2, NZ)), dma((1 + NZ,)),
            dma((4, 3)), dma((4, 3)),
            dma((2, 4)), dma((2, 4)),
        ],
        compiler_params=pltpu.CompilerParams(
            collective_id=cid, has_side_effects=True, vmem_limit_bytes=56 * 2**20
        ),
    )(
        features,
        norm_gain_weight.reshape(1, ch),
        norm_bias.reshape(1, ch),
        kernel.reshape(27, ch, ch),
        cotangent,
    )


def on_device(features, norm_gain_weight, norm_bias, kernel, cotangent):
    ch = features.shape[-1]
    fg, gk, gs = call(0, 0, features, norm_gain_weight, norm_bias, kernel, cotangent)
    taps = jnp.transpose(gk, (0, 1, 4, 2, 3, 5, 6)).reshape(4 * HALF, ch, ch)[: LAST + 1]
    return fg, taps.reshape(3, 3, 3, ch, ch), gs[0], gs[1]


def solution(mesh):
    placed = (P("frame", "tile", None, None), P(), P(), P(), P("frame", "tile", None, None))
    return jax.shard_map(
        on_device,
        mesh=mesh,
        in_specs=placed,
        out_specs=(P("frame", "tile", None, None), P(), P(), P()),
        check_vma=False,
    )
```

time: 863 us -> 79.8 us (0.09)
  waiting for transfers between devices: 473 us -> 0 us
  blocking collectives: 311 us -> 0 us
  Pallas kernels: 0 us -> 74.7 us
  local copies, waits for them, and re-layouts: 25.6 us -> 4.34 us
  starting transfers between devices: 18 us -> 0 us
  between operations: 14.7 us -> 0.67 us
  other arithmetic: 13.6 us -> 0 us
    psum x1 -> x0, waiting for transfers between devices: 466 us -> none  [on_device(): grad_kernel = lax.psum(local_kernel, ('frame', 'tile'))]
    psum x3 -> x0, blocking collectives: 311 us -> none  [the longest x1 109 us: on_device(): lax.psum(jnp.sum(grouped, axis=(0, 2)), ('frame', 'tile')) / cell_count]
    pallas_call x0 -> x1, Pallas kernels: none -> 74.7 us  [call(): pl.pallas_call(functools.partial(body, stop), out_shape=(jax.ShapeDtypeSt...]
    ppermute x6 -> x0, starting transfers between devices: 17.9 us -> none  [the longest x2 8.51 us: padded(): lax.ppermute(tail, axis, [(i, (i + 1) % count) for i in range(ends)])]
    reshape x11 -> x0, local copies, waits for them, and re-layouts: 11 us -> none  [the longest x9 10.9 us: on_device(): patches = jnp.concatenate([act_full[frame_tap:frame_tap + frames, row_tap...]
    concatenate x15 -> x0, other arithmetic: 9.16 us -> none  [the longest x7 8.14 us: on_device(): jnp.concatenate([act_full[frame_tap:frame_tap + frames, row_tap:row_tap +...]
  transfers between devices with their start and end apart: 7 -> 0, of which waited for: 3 -> 0; matrix products, arithmetic and copies ran while one was open for 1% -> 0% of each run, Pallas kernels for 0% -> 0%
where the time goes in v2:
time: 79.8 us; the launch traced here: 79.7 us
  Pallas kernels  74.7 us (94%)
  local copies, waits for them, and re-layouts  4.34 us (5%)
    pallas_call x1, Pallas kernels, call(): pl.pallas_call(functools.partial(body, stop), out_shape=(jax.ShapeDtypeSt...  74.7 us
    transpose x1, local copies, waits for them, and re-layouts, on_device(): jnp.transpose(gk, (0, 1, 4, 2, 3, 5, 6)).reshape(4 * HALF, ch, ch)  1.74 us

profile of v2, /device:TPU:1, one launch (start us, length us, event | category | flops | bytes accessed | tf_op | source)
XLA Modules:
  0.0 79.7 jit_solution(8939152894295489474)
XLA Ops:
  0.6 74.7 %shard_map.84 = (bf16[2,6,64,128]{3,2,1,0:T(8,128)(2,1)}, f32[2,2,4,4,7,8,128]{6,5,4,3,2,1,0:T(8,128)}, f32[2,128]{1,0:T(2,128)}) custom-call(bf16[2,6,64,128]{3,2,1,0:T(8,128)(2,1)} %feat_h.1, f32[1,128]{1,0:T(1,128)} %bitcast.14, f32[1,128]{1,0:T(1,128)} %bitcast.15, bf16[27,128,128]{2,1,0:T(8,128)(2,1)} %bitcast.13, bf16[2,6,64,128]{3,2,1,0:T(8,128)(2,1)} %cot_h.1), custom_call_target="tpu_custom_call" | custom-call | tf_op jit(solution)/shard_map/pallas_call | solution.py:438
  75.3 1.7 %copy.9 = f32[2,2,7,4,4,8,128]{6,5,4,3,2,1,0:T(8,128)S(1)} copy(f32[2,2,7,4,4,8,128]{6,5,2,4,3,1,0:T(8,128)} %bitcast.11) | data formatting | bytes 3670016 | tf_op jit(solution)/shard_map/transpose | solution.py:492
  77.1 0.0 copy-start.1
  77.1 0.0 copy-start
  77.1 1.4 %slice.12 = f32[27,128,128]{2,1,0:T(8,128)} slice(f32[28,128,128]{2,1,0:T(8,128)S(1)} %bitcast.10), slice={[0:27], [0:128], [0:128]} | slice | bytes 3538944 | tf_op jit(solution)/shard_map/slice | solution.py:492
  78.5 0.0 copy-done.1
  78.5 0.5 slice_bitcast_fusion
  79.0 0.0 copy-done
  79.0 0.7 copy.11
Async XLA Ops:
  77.1 1.4 %copy-start.1 = (f32[2,128]{1,0:T(2,128)S(1)}, f32[2,128]{1,0:T(2,128)}, u32[]{:S(2)}) copy-start(f32[2,128]{1,0:T(2,128)} %get-tuple-element.9) | copy-start | bytes 3076
  77.1 1.9 %copy-start = (bf16[2,6,64,128]{3,2,1,0:T(8,128)(2,1)S(1)}, bf16[2,6,64,128]{3,2,1,0:T(8,128)(2,1)}, u32[]{:S(2)}) copy-start(bf16[2,6,64,128]{3,2,1,0:T(8,128)(2,1)} %get-tuple-element.16) | copy-start | bytes 589828

commit v3 on v2

--- a/solution.py
+++ b/solution.py
@@ -37,10 +37,10 @@
     stop,
     feat_h, gain_h, bias_h, w_h, cot_h,
     fg, gk, gs,
-    fx, gain, bias, w, ext, cotx, gact, xhat, act_t,
+    fx, gain, bias, w, ext, cotx, gact, xhat, feat_t, act_t,
     s0, s1, s2, g0, g1, g2,
     part, ra1, rb1, ra2, rb2, zsrc, rz,
-    load_s, halo_s, halo_r, sm_s, sm_r, st_s, st_r, z_s, z_r, ag_s, ag_r, fw_s, fw_r,
+    load_s, halo_s, halo_r, sm_s, sm_r, rs_s, rs_r1, rs_r2, z_s, z_r, ag_s, ag_r1, ag_r2, fw_s, fw_r,
 ):
     f, t = lax.axis_index("frame"), lax.axis_index("tile")
     y, x = f // NX, lax.rem(f, NX)
@@ -200,6 +200,13 @@
         cotx[1, p, r] = ext[p, r]
         cotx[2, p, r] = down.astype(BF16)
 
+    @pl.loop(0, 2 * chunks)
+    def _(k):
+        c, kk = k // chunks, lax.rem(k, chunks)
+        per = chunks // frames
+        to = (kk // per) * (2 * per) + c * per + lax.rem(kk, per)
+        feat_t[to] = flat[c, pl.ds(kk * CHUNK, CHUNK), :].T
+
     for c in loads[2:]:
         c.wait()
     gact[...] = jnp.zeros_like(gact)
@@ -230,14 +237,15 @@
         nrm = xh * gw + bw
         return xh, nrm, 1.0 / (1.0 + jnp.exp(-nrm))
 
+    def down(v):
+        return jnp.broadcast_to(v, (CHUNK, ch)).T
+
+    avg_t, scale_t, bias_t = down(g_avg), down(inv * gw), down(bw)
+
     @pl.loop(0, 2 * chunks)
     def _(k):
-        c, kk = k // chunks, lax.rem(k, chunks)
-        _, nrm, s = normed(c, kk)
-        act = (nrm * s).astype(BF16)
-        per = chunks // frames
-        to = (kk // per) * (2 * per) + c * per + lax.rem(kk, per)
-        act_t[to] = act.T
+        nrm = (feat_t[k].astype(F32) - avg_t) * scale_t + bias_t
+        act_t[k] = (nrm * (1.0 / (1.0 + jnp.exp(-nrm)))).astype(BF16)
 
     def pair(q):
         got = []
@@ -254,19 +262,14 @@
             part[j // HALF, :, :, lax.rem(j, HALF)] = out[:, n * ch : (n + 1) * ch].reshape(NX, NY, 8, ch)
 
     pl.loop(0, 4)(pair)
-    a1 = [
-        rcopy(part.at[0, xo], ra1.at[i], st_s.at[0, i], st_r.at[0, i], dev)
-        for i, (xo, dev) in enumerate(zip(xs, xdevs))
-    ]
-    for c in a1:
-        c.start()
+    def pieces_out(h, order, take, devs, into):
+        for p, o in enumerate(order):
+            for i, (to, dev) in enumerate(devs):
+                rcopy(take(to, o), into.at[p, i], rs_s.at[0], rs_r1.at[h, p], dev).start()
+
+    pieces_out(0, ys + [y], lambda to, o: part.at[0, to, o], list(zip(xs, xdevs)), ra1)
     pl.loop(4, HALF)(pair)
-    b1 = [
-        rcopy(part.at[1, :, yo], rb1.at[i], st_s.at[1, i], st_r.at[1, i], dev)
-        for i, (yo, dev) in enumerate(zip(ys, ydevs))
-    ]
-    for c in b1:
-        c.start()
+    pieces_out(1, xs + [x], lambda to, o: part.at[1, o, to], list(zip(ys, ydevs)), rb1)
 
     def norm_grad(k, acc):
         at_rows = pl.ds(k * CHUNK, CHUNK)
@@ -294,26 +297,16 @@
 
     pass_on(g0, 3, 1, g1, f, fdevs)
 
-    for c in a1:
-        c.wait_recv()
-    part[0, x] += ra1[0] + ra1[1] + ra1[2]
-    a2 = [
-        rcopy(part.at[0, x, yo], ra2.at[i], st_s.at[2, i], st_r.at[2, i], dev)
-        for i, (yo, dev) in enumerate(zip(ys, ydevs))
-    ]
-    for c in a2:
-        c.start()
-    for c in b1:
-        c.wait_recv()
-    part[1, :, y] += rb1[0] + rb1[1] + rb1[2]
-    b2 = [
-        rcopy(part.at[1, xo, y], rb2.at[i], st_s.at[3, i], st_r.at[3, i], dev)
-        for i, (xo, dev) in enumerate(zip(xs, xdevs))
-    ]
-    for c in b2:
-        c.start()
-
-    pass_on(g1, 4, NF - 1, g2, z, zdevs)
+    for p in range(NX):
+        yo, xo = (ys + [y])[p], (xs + [x])[p]
+        rcopy(ra1.at[p], ra1.at[p], rs_s.at[0], rs_r1.at[0, p], mate).wait_recv()
+        part[0, x, yo] += ra1[p, 0] + ra1[p, 1] + ra1[p, 2]
+        if p < NX - 1:
+            rcopy(part.at[0, x, yo], ra2.at[p], rs_s.at[0], rs_r2.at[0], ydevs[p]).start()
+        rcopy(rb1.at[p], rb1.at[p], rs_s.at[0], rs_r1.at[1, p], mate).wait_recv()
+        part[1, xo, y] += rb1[p, 0] + rb1[p, 1] + rb1[p, 2]
+        if p < NX - 1:
+            rcopy(part.at[1, xo, y], rb2.at[p], rs_s.at[0], rs_r2.at[1], xdevs[p]).start()
 
     def z_send(h):
         for j in range(HALF):
@@ -321,31 +314,33 @@
 
             @pl.when(z != q)
             def _():
-                rcopy(zsrc.at[h, j], rz.at[z], z_s.at[0, q], z_r.at[0], (f, q * 2 + core)).start()
-
-    for c in a2:
-        c.wait_recv()
+                rcopy(zsrc.at[h, j], rz.at[z], z_s.at[0], z_r.at[0], (f, q * 2 + core)).start()
+
+    rcopy(ra2, ra2, rs_s.at[0], rs_r2.at[0], mate).wait_recv()
     zsrc[0] = part[0, x, y] + (ra2[0] + ra2[1] + ra2[2])
     z_send(0)
-    for c in b2:
-        c.wait_recv()
+    rcopy(rb2, rb2, rs_s.at[0], rs_r2.at[1], mate).wait_recv()
     zsrc[1] = part[1, x, y] + (rb2[0] + rb2[1] + rb2[2])
     z_send(1)
-    for c in a1 + b1 + a2 + b2:
-        c.wait_send()
+
+    pass_on(g1, 4, NF - 1, g2, z, zdevs)
+    sent = part.reshape(2 * NX * NY, HALF, 8, ch).at[pl.ds(0, 30)]
+    rcopy(sent, sent, rs_s.at[0], rs_r2.at[0], mate).wait_send()
 
     full = gk.at[core]
     mine = full.at[:, x, y]
+
+    def tiles(n):
+        return rz.at[pl.ds(0, n)]
 
     @pl.when(z < 2 * HALF)
     def _():
         h, j = lax.rem(z, 2), z // 2
         rz[z] = zsrc[h, j]
-        many = rz.at[pl.ds(0, NZ - 1)]
-        rcopy(many, many, z_s.at[0, 0], z_r.at[0], mate).wait_recv()
+        rcopy(tiles(NZ - 1), tiles(NZ - 1), z_s.at[0], z_r.at[0], mate).wait_recv()
         mine[h, j] = jnp.sum(rz[...], axis=0)
-        for jz, dev in zip(zs, zdevs):
-            rcopy(mine.at[h, j], mine.at[h, j], z_s.at[1, jz], z_r.at[1 + z], dev).start()
+        for dev in zdevs:
+            rcopy(mine.at[h, j], mine.at[h, j], z_s.at[1], z_r.at[1 + h], dev).start()
 
     fan_recv(g2, 5, NZ - 1)
     fan_sent(g2, 5, NZ - 1)
@@ -365,67 +360,81 @@
             inv * (gact[at_rows, :] * gw - g_mean - xhat[at_rows, :] * g_proj)
         ).astype(BF16)
 
-    for h in range(2):
-        for j in range(HALF):
-            q = 2 * j + h
-
-            @pl.when(z != q)
-            def _():
-                rcopy(zsrc.at[h, j], rz.at[z], z_s.at[0, q], z_r.at[0], (f, q * 2 + core)).wait_send()
-
     def z_recv(h):
-        for j in range(HALF):
-            q = 2 * j + h
-
-            @pl.when(z != q)
-            def _():
-                rcopy(mine.at[h, j], mine.at[h, j], z_s.at[1, 0], z_r.at[1 + q], mate).wait_recv()
-
-    def gather(here, there, k, devs):
-        sends = [rcopy(here, here, ag_s.at[k, i], ag_r.at[k, i], dev) for i, dev in enumerate(devs)]
-        come = [rcopy(p, p, ag_s.at[k, i], ag_r.at[k, i], mate) for i, p in enumerate(there)]
-        for c in sends:
-            c.start()
-        return sends, come
+        own = jnp.logical_and(z < 2 * HALF, lax.rem(z, 2) == h)
+
+        @pl.when(own)
+        def _():
+            rcopy(tiles(HALF - 1), tiles(HALF - 1), z_s.at[1], z_r.at[1 + h], mate).wait_recv()
+
+        @pl.when(jnp.logical_not(own))
+        def _():
+            rcopy(tiles(HALF), tiles(HALF), z_s.at[1], z_r.at[1 + h], mate).wait_recv()
 
     def behind(v, n):
         return [lax.rem(v - i + n, n) for i in range(1, n)]
 
     xb, yb = behind(x, NX), behind(y, NY)
 
-    def forward(piece, h, i):
-        c = rcopy(piece, piece, fw_s.at[h, i], fw_r.at[h, i], mate)
-        c.start()
-        return c
-
-    z_recv(0)
-    a_out, a_in = gather(full.at[0, x, y], [full.at[0, x, i] for i in yb], 0, ydevs)
-    z_recv(1)
-    b_out, b_in = gather(full.at[1, x, y], [full.at[1, i, y] for i in xb], 1, xdevs)
-    for c in a_in:
-        c.wait_recv()
-    a_out2, a_in2 = gather(full.at[0, x], [full.at[0, i] for i in xb], 2, xdevs)
-    fw = [forward(full.at[0, x], 0, 0)]
-    for c in b_in:
-        c.wait_recv()
-    b_out2, b_in2 = gather(full.at[1, :, y], [full.at[1, :, i] for i in yb], 3, ydevs)
-    fw.append(forward(full.at[1, :, y], 1, 0))
-    for i in range(NX - 1):
-        a_in2[i].wait_recv()
-        fw.append(forward(full.at[0, xb[i]], 0, i + 1))
-        b_in2[i].wait_recv()
-        fw.append(forward(full.at[1, :, yb[i]], 1, i + 1))
+    def put(piece, sem, dev):
+        rcopy(piece, piece, ag_s.at[0], sem, dev).start()
+
+    def come(piece, sem):
+        rcopy(piece, piece, ag_s.at[0], sem, mate).wait_recv()
+
+    def forward(piece):
+        rcopy(piece, piece, fw_s.at[0], fw_r.at[0], mate).start()
+
+    places = [[(x, yy) for yy in [y] + yb], [(xx, y) for xx in [x] + xb]]
+    first_devs, second_devs = [ydevs, xdevs], [xdevs, ydevs]
+    for p in range(NX):
+        for h in range(2):
+            piece = full.at[h, places[h][p][0], places[h][p][1]]
+            if p == 0:
+                z_recv(h)
+                for i, dev in enumerate(first_devs[h]):
+                    put(piece, ag_r1.at[h, i], dev)
+            else:
+                come(piece, ag_r1.at[h, p - 1])
+            for i, dev in enumerate(second_devs[h]):
+                put(piece, ag_r2.at[h, p, i], dev)
+            forward(piece)
+    for p in range(NX):
+        for i in range(NX - 1):
+            for h in range(2):
+                px, py = places[h][p]
+                piece = full.at[0, xb[i], py] if h == 0 else full.at[1, px, yb[i]]
+                come(piece, ag_r2.at[h, p, i])
+                forward(piece)
 
     @pl.when(z < 2 * HALF)
     def _():
-        h, j = lax.rem(z, 2), z // 2
-        for jz, dev in zip(zs, zdevs):
-            rcopy(mine.at[h, j], mine.at[h, j], z_s.at[1, jz], z_r.at[1 + z], dev).wait_send()
-
-    for c in a_out + b_out + a_out2 + b_out2:
-        c.wait_send()
-    for c in fw:
+        rcopy(tiles(NZ - 1), tiles(NZ - 1), z_s.at[1], z_r.at[0], mate).wait_send()
+        rcopy(tiles(2 * HALF - 1), tiles(2 * HALF - 1), z_s.at[0], z_r.at[0], mate).wait_send()
+
+    @pl.when(z >= 2 * HALF)
+    def _():
+        rcopy(tiles(2 * HALF), tiles(2 * HALF), z_s.at[0], z_r.at[0], mate).wait_send()
+
+    rcopy(sent, sent, ag_s.at[0], ag_r1.at[0, 0], mate).wait_send()
+    rcopy(full, full, fw_s.at[0], fw_r.at[0], mate).wait_send()
+    rcopy(gk.at[other], gk.at[other], fw_s.at[0], fw_r.at[0], mate).wait_recv()
+
+
+def place(fg, gk, gs, fg_o, gk_o, gain_o, shift_o, sem):
+    copies = [
+        pltpu.make_async_copy(fg, fg_o, sem.at[0]),
+        pltpu.make_async_copy(gs.at[0:1], gain_o, sem.at[1]),
+        pltpu.make_async_copy(gs.at[1:2], shift_o, sem.at[2]),
+    ]
+    for tap in range(LAST + 1):
+        core, h, j = tap // (2 * HALF), tap // HALF % 2, tap % HALF
+        pltpu.make_async_copy(gk.at[core, h, :, :, j], gk_o.at[tap], sem.at[3]).start()
+    for c in copies:
+        c.start()
+    for c in copies:
         c.wait()
+    pltpu.make_async_copy(gk_o, gk_o, sem.at[3]).wait()
 
 
 def call(stop, cid, features, norm_gain_weight, norm_bias, kernel, cotangent):
@@ -454,6 +463,7 @@
             pltpu.VMEM((cells, ch), F32),
             pltpu.VMEM((cells, ch), F32),
             pltpu.VMEM((2 * cells // CHUNK, ch, CHUNK), BF16),
+            pltpu.VMEM((2 * cells // CHUNK, ch, CHUNK), BF16),
             pltpu.VMEM((2, 2, ch), F32),
             pltpu.VMEM((NF, 2, ch), F32),
             pltpu.VMEM((NZ, 2, ch), F32),
@@ -461,36 +471,54 @@
             pltpu.VMEM((NF, 2, ch), F32),
             pltpu.VMEM((NZ, 2, ch), F32),
             pltpu.VMEM((2, NX, NY, HALF) + tile, F32),
-            pltpu.VMEM((3, NY, HALF) + tile, F32),
-            pltpu.VMEM((3, NX, HALF) + tile, F32),
+            pltpu.VMEM((NY, 3, HALF) + tile, F32),
+            pltpu.VMEM((NX, 3, HALF) + tile, F32),
             pltpu.VMEM((3, HALF) + tile, F32),
             pltpu.VMEM((3, HALF) + tile, F32),
             pltpu.VMEM((2, HALF) + tile, F32),
             pltpu.VMEM((NZ,) + tile, F32),
             dma((5,)), dma((8,)), dma((8,)),
             dma((6,)), dma((6,)),
-            dma((4, 3)), dma((4, 3)),
-            dma((2, NZ)), dma((1 + NZ,)),
-            dma((4, 3)), dma((4, 3)),
-            dma((2, 4)), dma((2, 4)),
+            dma((1,)), dma((2, NX)), dma((2,)),
+            dma((2,)), dma((3,)),
+            dma((1,)), dma((2, 3)), dma((2, NX, 3)),
+            dma((1,)), dma((1,)),
         ],
         compiler_params=pltpu.CompilerParams(
-            collective_id=cid, has_side_effects=True, vmem_limit_bytes=56 * 2**20
+            collective_id=cid, has_side_effects=True, vmem_limit_bytes=24 * 2**20
         ),
     )(
-        features,
-        norm_gain_weight.reshape(1, ch),
-        norm_bias.reshape(1, ch),
-        kernel.reshape(27, ch, ch),
-        cotangent,
+        *(
+            pltpu.with_memory_space_constraint(v, pltpu.HBM)
+            for v in (
+                features,
+                norm_gain_weight.reshape(1, ch),
+                norm_bias.reshape(1, ch),
+                kernel.reshape(27, ch, ch),
+                cotangent,
+            )
+        )
     )
 
 
 def on_device(features, norm_gain_weight, norm_bias, kernel, cotangent):
     ch = features.shape[-1]
-    fg, gk, gs = call(0, 0, features, norm_gain_weight, norm_bias, kernel, cotangent)
-    taps = jnp.transpose(gk, (0, 1, 4, 2, 3, 5, 6)).reshape(4 * HALF, ch, ch)[: LAST + 1]
-    return fg, taps.reshape(3, 3, 3, ch, ch), gs[0], gs[1]
+    made = call(0, 0, features, norm_gain_weight, norm_bias, kernel, cotangent)
+    vm = pl.BlockSpec(memory_space=pltpu.VMEM)
+    hbm = pl.BlockSpec(memory_space=pltpu.HBM)
+    fg, taps, gain, shift = pl.pallas_call(
+        place,
+        out_shape=(
+            jax.ShapeDtypeStruct(features.shape, BF16),
+            jax.ShapeDtypeStruct((LAST + 1, NX, NY, 8, ch), F32),
+            jax.ShapeDtypeStruct((1, ch), F32),
+            jax.ShapeDtypeStruct((1, ch), F32),
+        ),
+        in_specs=[vm] * 3,
+        out_specs=(hbm,) * 4,
+        scratch_shapes=[pltpu.SemaphoreType.DMA((4,))],
+    )(*made)
+    return fg, taps.reshape(3, 3, 3, ch, ch), gain.reshape(ch), shift.reshape(ch)
 
 
 def solution(mesh):

time: 79.8 us -> 77.7 us (0.974)
  local copies, waits for them, and re-layouts: 4.34 us -> 2.5 us
    pallas_call x1, Pallas kernels: 74.7 us -> 71.6 us  [call(): pl.pallas_call(functools.partial(body, stop), out_shape=(jax.ShapeDtypeSt...]
    pallas_call x0 -> x1, Pallas kernels: none -> 2.78 us  [on_device(): pl.pallas_call(place, out_shape=(jax.ShapeDtypeStruct(features.shape, BF1...]
    unnamed x5 -> x6, local copies, waits for them, and re-layouts: 0.69 us -> 2.5 us
    transpose x1 -> x0, local copies, waits for them, and re-layouts: 1.74 us -> none  [on_device(): jnp.transpose(gk, (0, 1, 4, 2, 3, 5, 6)).reshape(4 * HALF, ch, ch)]
    slice x1 -> x0, local copies, waits for them, and re-layouts: 1.4 us -> none  [on_device(): jnp.transpose(gk, (0, 1, 4, 2, 3, 5, 6)).reshape(4 * HALF, ch, ch)]
where the time goes in v3:
time: 77.7 us; the launch traced here: 77.5 us
  Pallas kernels  74.4 us (96%)
  local copies, waits for them, and re-layouts  2.5 us (3%)
    pallas_call x1, Pallas kernels, call(): pl.pallas_call(functools.partial(body, stop), out_shape=(jax.ShapeDtypeSt...  71.6 us
    pallas_call x1, Pallas kernels, on_device(): pl.pallas_call(place, out_shape=(jax.ShapeDtypeStruct(features.shape, BF1...  2.78 us
    unnamed x6, local copies, waits for them, and re-layouts  2.5 us

profile of v3, /device:TPU:1, one launch (start us, length us, event | category | flops | bytes accessed | tf_op | source)
XLA Modules:
  0.0 77.5 jit_solution(9146848704604989633)
XLA Ops:
  0.6 71.6 %shard_map.84 = (bf16[2,6,64,128]{3,2,1,0:T(8,128)(2,1)S(1)}, f32[2,2,4,4,7,8,128]{6,5,4,3,2,1,0:T(8,128)S(1)}, f32[2,128]{1,0:T(2,128)S(1)}) custom-call(bf16[2,6,64,128]{3,2,1,0:T(8,128)(2,1)} %feat_h.1, f32[1,128]{1,0:T(1,128)} %bitcast.7, f32[1,128]{1,0:T(1,128)} %bitcast.8, bf16[27,128,128]{2,1,0:T(8,128)(2,1)} %bitcast.6, bf16[2,6,64,128]{3,2,1,0:T(8,128)(2,1)} %cot_h.1), custom_call_target="tpu_custom_call" | custom-call | tf_op jit(solution)/shard_map/pallas_call | solution.py:447
  72.2 0.0 copy-start
  72.2 1.2 %copy-done = f32[2,2,4,4,7,8,128]{6,5,4,3,2,1,0:T(8,128)} copy-done((f32[2,2,4,4,7,8,128]{6,5,4,3,2,1,0:T(8,128)}, f32[2,2,4,4,7,8,128]{6,5,4,3,2,1,0:T(8,128)S(1)}, u32[]{:S(2)}) %copy-start) | copy-done | bytes 1835032
  73.5 0.0 copy-start.1
  73.5 0.7 copy-done.1
  74.1 0.0 copy-start.2
  74.1 0.6 copy-done.2
  74.7 2.8 %shard_map.85 = (bf16[2,6,64,128]{3,2,1,0:T(8,128)(2,1)}, f32[27,4,4,8,128]{4,3,2,1,0:T(8,128)}, f32[1,128]{1,0:T(1,128)}, f32[1,128]{1,0:T(1,128)}) custom-call(bf16[2,6,64,128]{3,2,1,0:T(8,128)(2,1)} %copy-done.1, f32[2,2,4,4,7,8,128]{6,5,4,3,2,1,0:T(8,128)} %copy-done, f32[2,128]{1,0:T(2,128)} %copy-done.2), custom_call_target="tpu_custom_call" | custom-call | tf_op jit(solution)/shard_map/pallas_call | solution.py:509
Async XLA Ops:
  72.2 1.3 %copy-start = (f32[2,2,4,4,7,8,128]{6,5,4,3,2,1,0:T(8,128)}, f32[2,2,4,4,7,8,128]{6,5,4,3,2,1,0:T(8,128)S(1)}, u32[]{:S(2)}) copy-start(f32[2,2,4,4,7,8,128]{6,5,4,3,2,1,0:T(8,128)S(1)} %get-tuple-element.12.gk) | copy-start | bytes 5505028
  73.5 0.7 copy-start.1
  74.1 0.6 copy-start.2

commit v4 on v3

--- a/solution.py
+++ b/solution.py
@@ -327,8 +327,10 @@
     sent = part.reshape(2 * NX * NY, HALF, 8, ch).at[pl.ds(0, 30)]
     rcopy(sent, sent, rs_s.at[0], rs_r2.at[0], mate).wait_send()
 
-    full = gk.at[core]
-    mine = full.at[:, x, y]
+    share = 2 * HALF * core
+
+    def out_piece(h, px, py):
+        return gk.at[pl.ds(share + h * HALF, HALF), px, py]
 
     def tiles(n):
         return rz.at[pl.ds(0, n)]
@@ -338,9 +340,10 @@
         h, j = lax.rem(z, 2), z // 2
         rz[z] = zsrc[h, j]
         rcopy(tiles(NZ - 1), tiles(NZ - 1), z_s.at[0], z_r.at[0], mate).wait_recv()
-        mine[h, j] = jnp.sum(rz[...], axis=0)
+        tile = gk.at[share + h * HALF + j, x, y]
+        tile[...] = jnp.sum(rz[...], axis=0)
         for dev in zdevs:
-            rcopy(mine.at[h, j], mine.at[h, j], z_s.at[1], z_r.at[1 + h], dev).start()
+            rcopy(tile, tile, z_s.at[1], z_r.at[1 + h], dev).start()
 
     fan_recv(g2, 5, NZ - 1)
     fan_sent(g2, 5, NZ - 1)
@@ -389,7 +392,7 @@
     first_devs, second_devs = [ydevs, xdevs], [xdevs, ydevs]
     for p in range(NX):
         for h in range(2):
-            piece = full.at[h, places[h][p][0], places[h][p][1]]
+            piece = out_piece(h, *places[h][p])
             if p == 0:
                 z_recv(h)
                 for i, dev in enumerate(first_devs[h]):
@@ -403,7 +406,7 @@
         for i in range(NX - 1):
             for h in range(2):
                 px, py = places[h][p]
-                piece = full.at[0, xb[i], py] if h == 0 else full.at[1, px, yb[i]]
+                piece = out_piece(0, xb[i], py) if h == 0 else out_piece(1, px, yb[i])
                 come(piece, ag_r2.at[h, p, i])
                 forward(piece)
 
@@ -417,24 +420,21 @@
         rcopy(tiles(2 * HALF), tiles(2 * HALF), z_s.at[0], z_r.at[0], mate).wait_send()
 
     rcopy(sent, sent, ag_s.at[0], ag_r1.at[0, 0], mate).wait_send()
-    rcopy(full, full, fw_s.at[0], fw_r.at[0], mate).wait_send()
-    rcopy(gk.at[other], gk.at[other], fw_s.at[0], fw_r.at[0], mate).wait_recv()
+    full = gk.at[pl.ds(share, 2 * HALF)]
+    rcopy(full, full, fw_s.at[0], fw_r.at[0], mate).wait()
 
 
 def place(fg, gk, gs, fg_o, gk_o, gain_o, shift_o, sem):
     copies = [
-        pltpu.make_async_copy(fg, fg_o, sem.at[0]),
-        pltpu.make_async_copy(gs.at[0:1], gain_o, sem.at[1]),
-        pltpu.make_async_copy(gs.at[1:2], shift_o, sem.at[2]),
+        pltpu.make_async_copy(gk.at[pl.ds(0, LAST + 1)], gk_o, sem.at[0]),
+        pltpu.make_async_copy(fg, fg_o, sem.at[1]),
+        pltpu.make_async_copy(gs.at[0:1], gain_o, sem.at[2]),
+        pltpu.make_async_copy(gs.at[1:2], shift_o, sem.at[3]),
     ]
-    for tap in range(LAST + 1):
-        core, h, j = tap // (2 * HALF), tap // HALF % 2, tap % HALF
-        pltpu.make_async_copy(gk.at[core, h, :, :, j], gk_o.at[tap], sem.at[3]).start()
     for c in copies:
         c.start()
     for c in copies:
         c.wait()
-    pltpu.make_async_copy(gk_o, gk_o, sem.at[3]).wait()
 
 
 def call(stop, cid, features, norm_gain_weight, norm_bias, kernel, cotangent):
@@ -447,9 +447,9 @@
     return pl.pallas_call(
         functools.partial(body, stop),
         out_shape=(
-            jax.ShapeDtypeStruct(features.shape, BF16),
-            jax.ShapeDtypeStruct((2, 2, NX, NY, HALF) + tile, F32),
-            jax.ShapeDtypeStruct((2, ch), F32),
+            pltpu.VMEM(features.shape, BF16),
+            pltpu.VMEM((4 * HALF, NX, NY) + tile, F32),
+            pltpu.VMEM((2, ch), F32),
         ),
         in_specs=[hbm] * 5,
         out_specs=(vm, vm, vm),
@@ -517,7 +517,8 @@
         in_specs=[vm] * 3,
         out_specs=(hbm,) * 4,
         scratch_shapes=[pltpu.SemaphoreType.DMA((4,))],
-    )(*made)
+        compiler_params=pltpu.CompilerParams(vmem_limit_bytes=4 * 2**20),
+    )(*(pltpu.with_memory_space_constraint(v, pltpu.VMEM) for v in made))
     return fg, taps.reshape(3, 3, 3, ch, ch), gain.reshape(ch), shift.reshape(ch)
 
 

time: 77.7 us -> 73.4 us (0.945)
  local copies, waits for them, and re-layouts: 2.5 us -> 0 us
  Pallas kernels: 74.4 us -> 72.6 us
    unnamed x6 -> x0, local copies, waits for them, and re-layouts: 2.5 us -> none
    pallas_call x1, Pallas kernels: 2.78 us -> 1.3 us  [on_device(): pl.pallas_call(place, out_shape=(jax.ShapeDtypeStruct(features.shape, BF1...]
where the time goes in v4:
time: 73.4 us; the launch traced here: 73.3 us
  Pallas kernels  72.6 us (99%)
    pallas_call x1, Pallas kernels, call(): pl.pallas_call(functools.partial(body, stop), out_shape=(pltpu.VMEM(featu...  71.3 us

profile of v4, /device:TPU:1, one launch (start us, length us, event | category | flops | bytes accessed | tf_op | source)
XLA Modules:
  0.0 73.3 jit_solution(14525002289469271092)
XLA Ops:
  0.6 71.3 %shard_map.84 = (bf16[2,6,64,128]{3,2,1,0:T(8,128)(2,1)S(1)}, f32[28,4,4,8,128]{4,3,2,1,0:T(8,128)S(1)}, f32[2,128]{1,0:T(2,128)S(1)}) custom-call(bf16[2,6,64,128]{3,2,1,0:T(8,128)(2,1)} %feat_h.1, f32[1,128]{1,0:T(1,128)} %bitcast.7, f32[1,128]{1,0:T(1,128)} %bitcast.8, bf16[27,128,128]{2,1,0:T(8,128)(2,1)} %bitcast.6, bf16[2,6,64,128]{3,2,1,0:T(8,128)(2,1)} %cot_h.1), custom_call_target="tpu_custom_call" | custom-call | tf_op jit(solution)/shard_map/pallas_call | solution.py:447
  72.0 1.3 %shard_map.85 = (bf16[2,6,64,128]{3,2,1,0:T(8,128)(2,1)}, f32[27,4,4,8,128]{4,3,2,1,0:T(8,128)}, f32[1,128]{1,0:T(1,128)}, f32[1,128]{1,0:T(1,128)}) custom-call(bf16[2,6,64,128]{3,2,1,0:T(8,128)(2,1)S(1)} %get-tuple-element.11.fg, f32[28,4,4,8,128]{4,3,2,1,0:T(8,128)S(1)} %get-tuple-element.12.gk, f32[2,128]{1,0:T(2,128)S(1)} %get-tuple-element.13.gs), custom_call_target="tpu_custom_call" | custom-call | tf_op jit(solution)/shard_map/pallas_call | solution.py:509

commit v5 on v4

--- a/solution.py
+++ b/solution.py
@@ -19,6 +19,7 @@
 F32 = jnp.float32
 BF16 = jnp.bfloat16
 CHUNK = 128
+REACH = NZ // 4
 
 
 def group_sum(v):
@@ -38,9 +39,9 @@
     feat_h, gain_h, bias_h, w_h, cot_h,
     fg, gk, gs,
     fx, gain, bias, w, ext, cotx, gact, xhat, feat_t, act_t,
-    s0, s1, s2, g0, g1, g2,
+    s1, s2, g0, g1, g2,
     part, ra1, rb1, ra2, rb2, zsrc, rz,
-    load_s, halo_s, halo_r, sm_s, sm_r, rs_s, rs_r1, rs_r2, z_s, z_r, ag_s, ag_r1, ag_r2, fw_s, fw_r,
+    load_s, halo_s, halo_r, sm_s, sm_r, rs_s, rs_r1, rs_r2, z_s, z_r, ag_s, ag_r1, ag_r2, fw_s, fw_r, known,
 ):
     f, t = lax.axis_index("frame"), lax.axis_index("tile")
     y, x = f // NX, lax.rem(f, NX)
@@ -51,6 +52,7 @@
     mate = (f, z * 2 + other)
     zn = lax.rem(z - 1 + 2 * core + NZ, NZ)
     fdevs = [(lax.rem(f + i, NF), t) for i in range(1, NF)]
+    fboth = [mate] + [(dev[0], z * 2 + c) for dev in fdevs for c in (core, other)]
     far = sorted(range(1, NZ), key=lambda i: -min(i, NZ - i))
     zs = [lax.rem(z + i, NZ) for i in far]
     zdevs = [(f, j * 2 + core) for j in zs]
@@ -72,7 +74,9 @@
         c.start()
 
     barrier = pltpu.get_barrier_semaphore()
-    greet = zdevs + fdevs + [mate, (f, zn * 2 + other)]
+    near = [dev for i, dev in zip(far, zdevs) if min(i, NZ - i) <= REACH]
+    edge = [dev for i, dev in zip(far, zdevs) if min(i, NZ - i) == REACH]
+    greet = near + fboth + [(f, zn * 2 + other)]
     for dev in greet:
         pl.semaphore_signal(barrier, inc=1, device_id=dev, device_id_type=MESH)
 
@@ -90,8 +94,8 @@
         return acc + jnp.sum(d * d, axis=0, keepdims=True)
 
     m2 = lax.fori_loop(0, chunks, add_sq, jnp.zeros((1, ch), F32))
-    s0[core, 0:1, :] = mean
-    s0[core, 1:2, :] = m2
+    s1[core, f, 0:1, :] = mean
+    s1[core, f, 1:2, :] = m2
     loads[1].wait()
 
     pl.semaphore_wait(barrier, len(greet))
@@ -112,7 +116,10 @@
         many = buf.at[pl.ds(0, n)]
         rcopy(many, many, sm_s.at[k], sm_r.at[k], mate).wait_send()
 
-    fan(s0, core, [mate], 0)
+    for dev in fboth:
+        rcopy(s1.at[core, f], s1.at[core, f], sm_s.at[1], sm_r.at[1], dev).start()
+    for dev in edge:
+        pl.semaphore_signal(known, inc=1, device_id=dev, device_id_type=MESH)
     block = ext.at[0:2, own_rows]
     to_mate = rcopy(block, block, halo_s.at[0], halo_r.at[0], mate)
     feats = rcopy(fx.at[core], fx.at[core], halo_s.at[1], halo_r.at[1], mate)
@@ -136,12 +143,6 @@
             d * d, axis=0, keepdims=True
         )
 
-    fan_recv(s0, 0, 1)
-    avg, m2 = combine(s0, float(cells))
-    s1[f, 0:1, :] = avg
-    s1[f, 1:2, :] = m2
-    fan(s1, f, fdevs, 1)
-
     before = (lax.rem(f - 1 + NF, NF), t)
     later = ext.at[2:4, own_rows]
     to_before = rcopy(block, later, halo_s.at[4], halo_r.at[4], before)
@@ -165,25 +166,34 @@
     for c in rims:
         c.start()
 
-    fan_recv(s1, 1, NF - 1)
-    avg, m2 = combine(s1, float(cells * 2))
+    s1 = s1.reshape(2 * NF, 2, ch)
+    fan_recv(s1, 1, 2 * NF - 1)
+    avg, m2 = combine(s1, float(cells))
     s2[z, 0:1, :] = avg
     s2[z, 1:2, :] = m2
+    pl.semaphore_wait(known, len(edge))
     fan(s2, z, zdevs, 2)
 
     to_before.wait_recv()
     relay = rcopy(later, later, halo_s.at[7], halo_r.at[7], mate)
     relay.start()
+    feats.wait()
+
+    @pl.loop(0, 2 * chunks)
+    def _(k):
+        c, kk = k // chunks, lax.rem(k, chunks)
+        per = chunks // frames
+        to = (kk // per) * (2 * per) + c * per + lax.rem(kk, per)
+        feat_t[to] = flat[c, pl.ds(kk * CHUNK, CHUNK), :].T
+
     to_mate.wait()
-    feats.wait()
     for c in edges:
         c.wait_send()
     to_before.wait_send()
     for c in rims:
         c.wait()
     relay.wait()
-    fan_sent(s0, 0, 1)
-    fan_sent(s1, 1, NF - 1)
+    fan_sent(s1, 1, 2 * NF - 1)
 
     @pl.when(f == NF - 1)
     def _():
@@ -200,27 +210,10 @@
         cotx[1, p, r] = ext[p, r]
         cotx[2, p, r] = down.astype(BF16)
 
-    @pl.loop(0, 2 * chunks)
-    def _(k):
-        c, kk = k // chunks, lax.rem(k, chunks)
-        per = chunks // frames
-        to = (kk // per) * (2 * per) + c * per + lax.rem(kk, per)
-        feat_t[to] = flat[c, pl.ds(kk * CHUNK, CHUNK), :].T
-
+    fan_recv(s2, 2, NZ - 1)
+    fan_sent(s2, 2, NZ - 1)
     for c in loads[2:]:
         c.wait()
-    gact[...] = jnp.zeros_like(gact)
-
-    @pl.loop(0, 9)
-    def _(k):
-        a, b = k // 3, lax.rem(k, 3)
-        p, r = pl.ds(2 - a, frames), pl.ds(2 - b + rows * core, rows)
-        taps = jnp.concatenate([w[3 * k], w[3 * k + 1], w[3 * k + 2]], axis=1)
-        patch = jnp.concatenate([cotx[e, p, r].reshape(cells, ch) for e in range(3)], axis=1)
-        gact[...] += lax.dot_general(patch, taps, (((1,), (1,)), ((), ())), preferred_element_type=F32)
-
-    fan_recv(s2, 2, NZ - 1)
-    fan_sent(s2, 2, NZ - 1)
     if stop == 2:
         return
     avg, m2 = combine(s2, float(cells * 2 * NF))
@@ -270,6 +263,16 @@
     pieces_out(0, ys + [y], lambda to, o: part.at[0, to, o], list(zip(xs, xdevs)), ra1)
     pl.loop(4, HALF)(pair)
     pieces_out(1, xs + [x], lambda to, o: part.at[1, o, to], list(zip(ys, ydevs)), rb1)
+
+    gact[...] = jnp.zeros_like(gact)
+
+    @pl.loop(0, 9)
+    def _(k):
+        a, b = k // 3, lax.rem(k, 3)
+        p, r = pl.ds(2 - a, frames), pl.ds(2 - b + rows * core, rows)
+        taps = jnp.concatenate([w[3 * k], w[3 * k + 1], w[3 * k + 2]], axis=1)
+        patch = jnp.concatenate([cotx[e, p, r].reshape(cells, ch) for e in range(3)], axis=1)
+        gact[...] += lax.dot_general(patch, taps, (((1,), (1,)), ((), ())), preferred_element_type=F32)
 
     def norm_grad(k, acc):
         at_rows = pl.ds(k * CHUNK, CHUNK)
@@ -464,8 +467,7 @@
             pltpu.VMEM((cells, ch), F32),
             pltpu.VMEM((2 * cells // CHUNK, ch, CHUNK), BF16),
             pltpu.VMEM((2 * cells // CHUNK, ch, CHUNK), BF16),
-            pltpu.VMEM((2, 2, ch), F32),
-            pltpu.VMEM((NF, 2, ch), F32),
+            pltpu.VMEM((2, NF, 2, ch), F32),
             pltpu.VMEM((NZ, 2, ch), F32),
             pltpu.VMEM((2, 2, ch), F32),
             pltpu.VMEM((NF, 2, ch), F32),
@@ -483,6 +485,7 @@
             dma((2,)), dma((3,)),
             dma((1,)), dma((2, 3)), dma((2, NX, 3)),
             dma((1,)), dma((1,)),
+            pltpu.SemaphoreType.REGULAR,
         ],
         compiler_params=pltpu.CompilerParams(
             collective_id=cid, has_side_effects=True, vmem_limit_bytes=24 * 2**20

time: 73.4 us -> 68 us (0.926)
  Pallas kernels: 72.6 us -> 67.2 us
    pallas_call x1, Pallas kernels: 71.3 us -> 65.9 us  [call(): pl.pallas_call(functools.partial(body, stop), out_shape=(pltpu.VMEM(featu...]
where the time goes in v5:
time: 68 us; the launch traced here: 67.8 us
  Pallas kernels  67.2 us (99%)
    pallas_call x1, Pallas kernels, call(): pl.pallas_call(functools.partial(body, stop), out_shape=(pltpu.VMEM(featu...  65.9 us

profile of v5, /device:TPU:1, one launch (start us, length us, event | category | flops | bytes accessed | tf_op | source)
XLA Modules:
  0.0 67.8 jit_solution(13518643538898348326)
XLA Ops:
  0.6 65.9 %shard_map.84 = (bf16[2,6,64,128]{3,2,1,0:T(8,128)(2,1)S(1)}, f32[28,4,4,8,128]{4,3,2,1,0:T(8,128)S(1)}, f32[2,128]{1,0:T(2,128)S(1)}) custom-call(bf16[2,6,64,128]{3,2,1,0:T(8,128)(2,1)} %feat_h.1, f32[1,128]{1,0:T(1,128)} %bitcast.7, f32[1,128]{1,0:T(1,128)} %bitcast.8, bf16[27,128,128]{2,1,0:T(8,128)(2,1)} %bitcast.6, bf16[2,6,64,128]{3,2,1,0:T(8,128)(2,1)} %cot_h.1), custom_call_target="tpu_custom_call" | custom-call | tf_op jit(solution)/shard_map/pallas_call | solution.py:450
  66.5 1.3 %shard_map.85 = (bf16[2,6,64,128]{3,2,1,0:T(8,128)(2,1)}, f32[27,4,4,8,128]{4,3,2,1,0:T(8,128)}, f32[1,128]{1,0:T(1,128)}, f32[1,128]{1,0:T(1,128)}) custom-call(bf16[2,6,64,128]{3,2,1,0:T(8,128)(2,1)S(1)} %get-tuple-element.11.fg, f32[28,4,4,8,128]{4,3,2,1,0:T(8,128)S(1)} %get-tuple-element.12.gk, f32[2,128]{1,0:T(2,128)S(1)} %get-tuple-element.13.gs), custom_call_target="tpu_custom_call" | custom-call | tf_op jit(solution)/shard_map/pallas_call | solution.py:512

commit v6 on v5

--- a/solution.py
+++ b/solution.py
@@ -19,6 +19,7 @@
 F32 = jnp.float32
 BF16 = jnp.bfloat16
 CHUNK = 128
+FIRST = NZ // 2 + 1
 REACH = NZ // 4
 
 
@@ -210,10 +211,16 @@
         cotx[1, p, r] = ext[p, r]
         cotx[2, p, r] = down.astype(BF16)
 
+    for c in loads[2:]:
+        c.wait()
+    gw, bw = gain[...], bias[...]
+
+    def down(v):
+        return jnp.broadcast_to(v, (CHUNK, ch)).T
+
+    bias_t = down(bw)
     fan_recv(s2, 2, NZ - 1)
     fan_sent(s2, 2, NZ - 1)
-    for c in loads[2:]:
-        c.wait()
     if stop == 2:
         return
     avg, m2 = combine(s2, float(cells * 2 * NF))
@@ -223,19 +230,15 @@
     d = avg - g_avg
     spread = group_sum(m2 + per_channel * (d * d)) / (per_channel * group)
     inv = lax.rsqrt(spread + EPS)
-    gw, bw = gain[...], bias[...]
 
     def normed(c, k):
         xh = (flat[c, pl.ds(k * CHUNK, CHUNK), :].astype(F32) - g_avg) * inv
         nrm = xh * gw + bw
         return xh, nrm, 1.0 / (1.0 + jnp.exp(-nrm))
 
-    def down(v):
-        return jnp.broadcast_to(v, (CHUNK, ch)).T
-
-    avg_t, scale_t, bias_t = down(g_avg), down(inv * gw), down(bw)
-
-    @pl.loop(0, 2 * chunks)
+    avg_t, scale_t = down(g_avg), down(inv * gw)
+
+    @pl.loop(0, 2 * chunks, unroll=4)
     def _(k):
         nrm = (feat_t[k].astype(F32) - avg_t) * scale_t + bias_t
         act_t[k] = (nrm * (1.0 / (1.0 + jnp.exp(-nrm)))).astype(BF16)
@@ -254,19 +257,19 @@
             j = 2 * q + n
             part[j // HALF, :, :, lax.rem(j, HALF)] = out[:, n * ch : (n + 1) * ch].reshape(NX, NY, 8, ch)
 
-    pl.loop(0, 4)(pair)
+    pl.loop(0, 4, unroll=True)(pair)
     def pieces_out(h, order, take, devs, into):
         for p, o in enumerate(order):
             for i, (to, dev) in enumerate(devs):
                 rcopy(take(to, o), into.at[p, i], rs_s.at[0], rs_r1.at[h, p], dev).start()
 
     pieces_out(0, ys + [y], lambda to, o: part.at[0, to, o], list(zip(xs, xdevs)), ra1)
-    pl.loop(4, HALF)(pair)
+    pl.loop(4, HALF, unroll=True)(pair)
     pieces_out(1, xs + [x], lambda to, o: part.at[1, o, to], list(zip(ys, ydevs)), rb1)
 
     gact[...] = jnp.zeros_like(gact)
 
-    @pl.loop(0, 9)
+    @pl.loop(0, 9, unroll=3)
     def _(k):
         a, b = k // 3, lax.rem(k, 3)
         p, r = pl.ds(2 - a, frames), pl.ds(2 - b + rows * core, rows)
@@ -311,20 +314,19 @@
         if p < NX - 1:
             rcopy(part.at[1, xo, y], rb2.at[p], rs_s.at[0], rs_r2.at[1], xdevs[p]).start()
 
-    def z_send(h):
-        for j in range(HALF):
-            q = 2 * j + h
-
-            @pl.when(z != q)
-            def _():
-                rcopy(zsrc.at[h, j], rz.at[z], z_s.at[0], z_r.at[0], (f, q * 2 + core)).start()
-
     rcopy(ra2, ra2, rs_s.at[0], rs_r2.at[0], mate).wait_recv()
-    zsrc[0] = part[0, x, y] + (ra2[0] + ra2[1] + ra2[2])
-    z_send(0)
+    zsrc[0:HALF] = part[0, x, y] + (ra2[0] + ra2[1] + ra2[2])
     rcopy(rb2, rb2, rs_s.at[0], rs_r2.at[1], mate).wait_recv()
-    zsrc[1] = part[1, x, y] + (rb2[0] + rb2[1] + rb2[2])
-    z_send(1)
+    zsrc[HALF : 2 * HALF] = part[1, x, y] + (rb2[0] + rb2[1] + rb2[2])
+    for to, dev in zip(zs, zdevs):
+        q = lax.rem(to + NZ - FIRST, NZ)
+
+        @pl.when(q < 2 * HALF)
+        def _():
+            rcopy(zsrc.at[q], rz.at[z], z_s.at[0], z_r.at[0], dev).start()
+
+    owned = lax.rem(z + NZ - FIRST, NZ)
+    owner = owned < 2 * HALF
 
     pass_on(g1, 4, NF - 1, g2, z, zdevs)
     sent = part.reshape(2 * NX * NY, HALF, 8, ch).at[pl.ds(0, 30)]
@@ -338,15 +340,17 @@
     def tiles(n):
         return rz.at[pl.ds(0, n)]
 
-    @pl.when(z < 2 * HALF)
+    @pl.when(owner)
     def _():
-        h, j = lax.rem(z, 2), z // 2
-        rz[z] = zsrc[h, j]
+        rz[z] = zsrc[owned]
         rcopy(tiles(NZ - 1), tiles(NZ - 1), z_s.at[0], z_r.at[0], mate).wait_recv()
-        tile = gk.at[share + h * HALF + j, x, y]
+        tile = gk.at[share + owned, x, y]
         tile[...] = jnp.sum(rz[...], axis=0)
-        for dev in zdevs:
-            rcopy(tile, tile, z_s.at[1], z_r.at[1 + h], dev).start()
+        for i in sorted(range(NZ), key=lambda i: min(i, NZ - i)):
+
+            @pl.when(z != i)
+            def _():
+                rcopy(tile, tile, z_s.at[1], z_r.at[1 + owned // HALF], (f, i * 2 + core)).start()
 
     fan_recv(g2, 5, NZ - 1)
     fan_sent(g2, 5, NZ - 1)
@@ -367,7 +371,7 @@
         ).astype(BF16)
 
     def z_recv(h):
-        own = jnp.logical_and(z < 2 * HALF, lax.rem(z, 2) == h)
+        own = jnp.logical_and(owner, owned // HALF == h)
 
         @pl.when(own)
         def _():
@@ -406,19 +410,19 @@
                 put(piece, ag_r2.at[h, p, i], dev)
             forward(piece)
     for p in range(NX):
-        for i in range(NX - 1):
+        for i in (0, 2, 1):
             for h in range(2):
                 px, py = places[h][p]
                 piece = out_piece(0, xb[i], py) if h == 0 else out_piece(1, px, yb[i])
                 come(piece, ag_r2.at[h, p, i])
                 forward(piece)
 
-    @pl.when(z < 2 * HALF)
+    @pl.when(owner)
     def _():
         rcopy(tiles(NZ - 1), tiles(NZ - 1), z_s.at[1], z_r.at[0], mate).wait_send()
         rcopy(tiles(2 * HALF - 1), tiles(2 * HALF - 1), z_s.at[0], z_r.at[0], mate).wait_send()
 
-    @pl.when(z >= 2 * HALF)
+    @pl.when(jnp.logical_not(owner))
     def _():
         rcopy(tiles(2 * HALF), tiles(2 * HALF), z_s.at[0], z_r.at[0], mate).wait_send()
 
@@ -477,7 +481,7 @@
             pltpu.VMEM((NX, 3, HALF) + tile, F32),
             pltpu.VMEM((3, HALF) + tile, F32),
             pltpu.VMEM((3, HALF) + tile, F32),
-            pltpu.VMEM((2, HALF) + tile, F32),
+            pltpu.VMEM((2 * HALF,) + tile, F32),
             pltpu.VMEM((NZ,) + tile, F32),
             dma((5,)), dma((8,)), dma((8,)),
             dma((6,)), dma((6,)),

time: 68 us -> 66.2 us (0.974)
  Pallas kernels: 67.2 us -> 65.4 us
    pallas_call x1, Pallas kernels: 65.9 us -> 64.1 us  [call(): pl.pallas_call(functools.partial(body, stop), out_shape=(pltpu.VMEM(featu...]
where the time goes in v6:
time: 66.2 us; the launch traced here: 66.1 us
  Pallas kernels  65.4 us (99%)
    pallas_call x1, Pallas kernels, call(): pl.pallas_call(functools.partial(body, stop), out_shape=(pltpu.VMEM(featu...  64.1 us

profile of v6, /device:TPU:1, one launch (start us, length us, event | category | flops | bytes accessed | tf_op | source)
XLA Modules:
  0.0 66.1 jit_solution(3753293649128819397)
XLA Ops:
  0.6 64.1 %shard_map.84 = (bf16[2,6,64,128]{3,2,1,0:T(8,128)(2,1)S(1)}, f32[28,4,4,8,128]{4,3,2,1,0:T(8,128)S(1)}, f32[2,128]{1,0:T(2,128)S(1)}) custom-call(bf16[2,6,64,128]{3,2,1,0:T(8,128)(2,1)} %feat_h.1, f32[1,128]{1,0:T(1,128)} %bitcast.7, f32[1,128]{1,0:T(1,128)} %bitcast.8, bf16[27,128,128]{2,1,0:T(8,128)(2,1)} %bitcast.6, bf16[2,6,64,128]{3,2,1,0:T(8,128)(2,1)} %cot_h.1), custom_call_target="tpu_custom_call" | custom-call | tf_op jit(solution)/shard_map/pallas_call | solution.py:454
  64.8 1.3 %shard_map.85 = (bf16[2,6,64,128]{3,2,1,0:T(8,128)(2,1)}, f32[27,4,4,8,128]{4,3,2,1,0:T(8,128)}, f32[1,128]{1,0:T(1,128)}, f32[1,128]{1,0:T(1,128)}) custom-call(bf16[2,6,64,128]{3,2,1,0:T(8,128)(2,1)S(1)} %get-tuple-element.11.fg, f32[28,4,4,8,128]{4,3,2,1,0:T(8,128)S(1)} %get-tuple-element.12.gk, f32[2,128]{1,0:T(2,128)S(1)} %get-tuple-element.13.gs), custom_call_target="tpu_custom_call" | custom-call | tf_op jit(solution)/shard_map/pallas_call | solution.py:516

commit v7 on v6

--- a/solution.py
+++ b/solution.py
@@ -15,7 +15,10 @@
 NZ = 16
 NF = NX * NY
 LAST = 26
-HALF = 7
+LENS = ((3, 3), (4, 4))
+SHARE = tuple(2 * sum(n) for n in LENS)
+BASE = (0, SHARE[0])
+FROM = tuple(((0, n), (2 * n, 2 * n + m)) for n, m in LENS)
 F32 = jnp.float32
 BF16 = jnp.bfloat16
 CHUNK = 128
@@ -41,7 +44,7 @@
     fg, gk, gs,
     fx, gain, bias, w, ext, cotx, gact, xhat, feat_t, act_t,
     s1, s2, g0, g1, g2,
-    part, ra1, rb1, ra2, rb2, zsrc, rz,
+    part00, part01, part10, part11, ra00, ra01, ra10, ra11, rb00, rb01, rb10, rb11, zsrc, rz,
     load_s, halo_s, halo_r, sm_s, sm_r, rs_s, rs_r1, rs_r2, z_s, z_r, ag_s, ag_r1, ag_r2, fw_s, fw_r, known,
 ):
     f, t = lax.axis_index("frame"), lax.axis_index("tile")
@@ -243,192 +246,214 @@
         nrm = (feat_t[k].astype(F32) - avg_t) * scale_t + bias_t
         act_t[k] = (nrm * (1.0 / (1.0 + jnp.exp(-nrm)))).astype(BF16)
 
-    def pair(q):
-        got = []
-        for n in range(2):
-            tap = jnp.minimum(core * (2 * HALF) + 2 * q + n, LAST)
-            a, b, e = tap // 9, lax.rem(tap // 3, 3), lax.rem(tap, 3)
-            got.append(
-                cotx[e, pl.ds(2 - a, frames), pl.ds(2 - b, 2 * rows)].reshape(2 * cells, ch)
+    def finish(who):
+        parts = [[part00, part01], [part10, part11]][who]
+        ra = [[ra00, ra01], [ra10, ra11]][who]
+        rb = [[rb00, rb01], [rb10, rb11]][who]
+        lens, first, share, base = LENS[who], FROM[who], SHARE[who], BASE[who]
+        early, late = [x, y], [y, x]
+
+        def early_dev(h, i):
+            return (y * NX + lax.rem(x + i, NX), t) if h == 0 else (lax.rem(y + i, NY) * NX + x, t)
+
+        def late_dev(h, i):
+            return early_dev(1 - h, i)
+
+        def row(ref, h, at):
+            return ref.at[h, at] if h == 0 else ref.at[h, :, at]
+
+        acts = jnp.concatenate([act_t[i] for i in range(2 * chunks)], axis=1)
+
+        def first_stage(g):
+            for j in range(lens[g]):
+                got = []
+                for h in range(2):
+                    tap = min(base + first[g][h] + j, LAST)
+                    a, b, e = tap // 9, tap // 3 % 3, tap % 3
+                    got.append(
+                        cotx[e, pl.ds(2 - a, frames), pl.ds(2 - b, 2 * rows)].reshape(2 * cells, ch)
+                    )
+                out = jnp.dot(acts, jnp.concatenate(got, axis=1), preferred_element_type=F32)
+                for h in range(2):
+                    parts[g][h, :, :, j] = out[:, h * ch : (h + 1) * ch].reshape(NX, NY, 8, ch)
+            for h in range(2):
+                for i in (2, 1, 3):
+                    to = lax.rem(early[h] + i, NX)
+                    rcopy(
+                        row(parts[g], h, to), ra[g].at[h, i - 1], rs_s.at[g], rs_r1.at[g, h], early_dev(h, i)
+                    ).start()
+
+        first_stage(0)
+        first_stage(1)
+
+        gact[...] = jnp.zeros_like(gact)
+
+        @pl.loop(0, 9, unroll=3)
+        def _(k):
+            a, b = k // 3, lax.rem(k, 3)
+            p, r = pl.ds(2 - a, frames), pl.ds(2 - b + rows * core, rows)
+            taps = jnp.concatenate([w[3 * k], w[3 * k + 1], w[3 * k + 2]], axis=1)
+            patch = jnp.concatenate([cotx[e, p, r].reshape(cells, ch) for e in range(3)], axis=1)
+            gact[...] += lax.dot_general(patch, taps, (((1,), (1,)), ((), ())), preferred_element_type=F32)
+
+        def norm_grad(k, acc):
+            at_rows = pl.ds(k * CHUNK, CHUNK)
+            xh, nrm, s = normed(core, k)
+            gn = gact[at_rows, :] * s * (1.0 + nrm * (1.0 - s))
+            gact[at_rows, :] = gn
+            xhat[at_rows, :] = xh
+            return (
+                acc[0] + jnp.sum(gn * xh, axis=0, keepdims=True),
+                acc[1] + jnp.sum(gn, axis=0, keepdims=True),
             )
-        acts = jnp.concatenate([act_t[i] for i in range(2 * chunks)], axis=1)
-        out = jnp.dot(acts, jnp.concatenate(got, axis=1), preferred_element_type=F32)
-        for n in range(2):
-            j = 2 * q + n
-            part[j // HALF, :, :, lax.rem(j, HALF)] = out[:, n * ch : (n + 1) * ch].reshape(NX, NY, 8, ch)
-
-    pl.loop(0, 4, unroll=True)(pair)
-    def pieces_out(h, order, take, devs, into):
-        for p, o in enumerate(order):
-            for i, (to, dev) in enumerate(devs):
-                rcopy(take(to, o), into.at[p, i], rs_s.at[0], rs_r1.at[h, p], dev).start()
-
-    pieces_out(0, ys + [y], lambda to, o: part.at[0, to, o], list(zip(xs, xdevs)), ra1)
-    pl.loop(4, HALF, unroll=True)(pair)
-    pieces_out(1, xs + [x], lambda to, o: part.at[1, o, to], list(zip(ys, ydevs)), rb1)
-
-    gact[...] = jnp.zeros_like(gact)
-
-    @pl.loop(0, 9, unroll=3)
-    def _(k):
-        a, b = k // 3, lax.rem(k, 3)
-        p, r = pl.ds(2 - a, frames), pl.ds(2 - b + rows * core, rows)
-        taps = jnp.concatenate([w[3 * k], w[3 * k + 1], w[3 * k + 2]], axis=1)
-        patch = jnp.concatenate([cotx[e, p, r].reshape(cells, ch) for e in range(3)], axis=1)
-        gact[...] += lax.dot_general(patch, taps, (((1,), (1,)), ((), ())), preferred_element_type=F32)
-
-    def norm_grad(k, acc):
-        at_rows = pl.ds(k * CHUNK, CHUNK)
-        xh, nrm, s = normed(core, k)
-        gn = gact[at_rows, :] * s * (1.0 + nrm * (1.0 - s))
-        gact[at_rows, :] = gn
-        xhat[at_rows, :] = xh
-        return (
-            acc[0] + jnp.sum(gn * xh, axis=0, keepdims=True),
-            acc[1] + jnp.sum(gn, axis=0, keepdims=True),
-        )
-
-    zero = jnp.zeros((1, ch), F32)
-    d_gain, d_shift = lax.fori_loop(0, chunks, norm_grad, (zero, zero))
-    g0[core, 0:1, :] = d_gain
-    g0[core, 1:2, :] = d_shift
-    fan(g0, core, [mate], 3)
-
-    def pass_on(buf, k, n, to, me, devs):
-        fan_recv(buf, k, n)
-        to[me, 0:1, :] = jnp.sum(buf[:, 0, :], axis=0, keepdims=True)
-        to[me, 1:2, :] = jnp.sum(buf[:, 1, :], axis=0, keepdims=True)
-        fan(to, me, devs, k + 1)
-        fan_sent(buf, k, n)
-
-    pass_on(g0, 3, 1, g1, f, fdevs)
-
-    for p in range(NX):
-        yo, xo = (ys + [y])[p], (xs + [x])[p]
-        rcopy(ra1.at[p], ra1.at[p], rs_s.at[0], rs_r1.at[0, p], mate).wait_recv()
-        part[0, x, yo] += ra1[p, 0] + ra1[p, 1] + ra1[p, 2]
-        if p < NX - 1:
-            rcopy(part.at[0, x, yo], ra2.at[p], rs_s.at[0], rs_r2.at[0], ydevs[p]).start()
-        rcopy(rb1.at[p], rb1.at[p], rs_s.at[0], rs_r1.at[1, p], mate).wait_recv()
-        part[1, xo, y] += rb1[p, 0] + rb1[p, 1] + rb1[p, 2]
-        if p < NX - 1:
-            rcopy(part.at[1, xo, y], rb2.at[p], rs_s.at[0], rs_r2.at[1], xdevs[p]).start()
-
-    rcopy(ra2, ra2, rs_s.at[0], rs_r2.at[0], mate).wait_recv()
-    zsrc[0:HALF] = part[0, x, y] + (ra2[0] + ra2[1] + ra2[2])
-    rcopy(rb2, rb2, rs_s.at[0], rs_r2.at[1], mate).wait_recv()
-    zsrc[HALF : 2 * HALF] = part[1, x, y] + (rb2[0] + rb2[1] + rb2[2])
-    for to, dev in zip(zs, zdevs):
-        q = lax.rem(to + NZ - FIRST, NZ)
-
-        @pl.when(q < 2 * HALF)
+
+        zero = jnp.zeros((1, ch), F32)
+        d_gain, d_shift = lax.fori_loop(0, chunks, norm_grad, (zero, zero))
+        g0[core, 0:1, :] = d_gain
+        g0[core, 1:2, :] = d_shift
+        fan(g0, core, [mate], 3)
+
+        def pass_on(buf, k, n, to, me, devs):
+            fan_recv(buf, k, n)
+            to[me, 0:1, :] = jnp.sum(buf[:, 0, :], axis=0, keepdims=True)
+            to[me, 1:2, :] = jnp.sum(buf[:, 1, :], axis=0, keepdims=True)
+            fan(to, me, devs, k + 1)
+            fan_sent(buf, k, n)
+
+        pass_on(g0, 3, 1, g1, f, fdevs)
+
+        def second_stage(g):
+            for h in range(2):
+                got = ra[g].at[h]
+                rcopy(got, got, rs_s.at[g], rs_r1.at[g, h], mate).wait_recv()
+                mine = row(parts[g], h, early[h])
+                mine[...] += got[0] + got[1] + got[2]
+                for i in (2, 1, 3):
+                    rcopy(
+                        mine.at[lax.rem(late[h] + i, NX)], rb[g].at[h, i - 1], rs_s.at[g], rs_r2.at[g, h],
+                        late_dev(h, i),
+                    ).start()
+
+        def z_stage(g):
+            for h in range(2):
+                got = rb[g].at[h]
+                rcopy(got, got, rs_s.at[g], rs_r2.at[g, h], mate).wait_recv()
+                zsrc[first[g][h] : first[g][h] + lens[g]] = parts[g][h, x, y] + (got[0] + got[1] + got[2])
+            for to, dev in zip(zs, zdevs):
+                q = lax.rem(to + NZ - FIRST, NZ)
+
+                @pl.when(jnp.logical_and(q >= first[g][0], q < first[g][0] + 2 * lens[g]))
+                def _():
+                    rcopy(zsrc.at[q], rz.at[z], z_s.at[0], z_r.at[0], dev).start()
+
+        second_stage(0)
+        second_stage(1)
+        z_stage(0)
+        z_stage(1)
+        owned = lax.rem(z + NZ - FIRST, NZ)
+        owner = owned < share
+
+        pass_on(g1, 4, NF - 1, g2, z, zdevs)
+        sent = [parts[g].reshape(2 * NX * NY, lens[g], 8, ch).at[pl.ds(0, 30)] for g in range(2)]
+        for g in range(2):
+            rcopy(sent[g], sent[g], rs_s.at[g], rs_r2.at[g, 0], mate).wait_send()
+
+        def out_taps(g, h):
+            return gk.at[pl.ds(base + first[g][h], lens[g])]
+
+        def tiles(n):
+            return rz.at[pl.ds(0, n)]
+
+        @pl.when(owner)
         def _():
-            rcopy(zsrc.at[q], rz.at[z], z_s.at[0], z_r.at[0], dev).start()
-
-    owned = lax.rem(z + NZ - FIRST, NZ)
-    owner = owned < 2 * HALF
-
-    pass_on(g1, 4, NF - 1, g2, z, zdevs)
-    sent = part.reshape(2 * NX * NY, HALF, 8, ch).at[pl.ds(0, 30)]
-    rcopy(sent, sent, rs_s.at[0], rs_r2.at[0], mate).wait_send()
-
-    share = 2 * HALF * core
-
-    def out_piece(h, px, py):
-        return gk.at[pl.ds(share + h * HALF, HALF), px, py]
-
-    def tiles(n):
-        return rz.at[pl.ds(0, n)]
-
-    @pl.when(owner)
-    def _():
-        rz[z] = zsrc[owned]
-        rcopy(tiles(NZ - 1), tiles(NZ - 1), z_s.at[0], z_r.at[0], mate).wait_recv()
-        tile = gk.at[share + owned, x, y]
-        tile[...] = jnp.sum(rz[...], axis=0)
-        for i in sorted(range(NZ), key=lambda i: min(i, NZ - i)):
-
-            @pl.when(z != i)
+            rz[z] = zsrc[owned]
+            rcopy(tiles(NZ - 1), tiles(NZ - 1), z_s.at[0], z_r.at[0], mate).wait_recv()
+            tile = gk.at[base + owned, x, y]
+            tile[...] = jnp.sum(rz[...], axis=0)
+            for dev in zdevs:
+                rcopy(tile, tile, z_s.at[1], z_r.at[1 + owned // first[1][0]], dev).start()
+
+        fan_recv(g2, 5, NZ - 1)
+        fan_sent(g2, 5, NZ - 1)
+        d_gain = jnp.sum(g2[:, 0, :], axis=0, keepdims=True)
+        d_shift = jnp.sum(g2[:, 1, :], axis=0, keepdims=True)
+        gs[0:1, :] = d_gain
+        gs[1:2, :] = d_shift
+        count = per_channel * group
+        g_mean = group_sum(gw * d_shift) / count
+        g_proj = group_sum(gw * d_gain) / count
+        out = fg.reshape(cells, ch)
+
+        @pl.loop(0, chunks)
+        def _(k):
+            at_rows = pl.ds(pl.multiple_of(k * CHUNK, CHUNK), CHUNK)
+            out[at_rows, :] = (
+                inv * (gact[at_rows, :] * gw - g_mean - xhat[at_rows, :] * g_proj)
+            ).astype(BF16)
+
+        def z_recv(g):
+            n = 2 * lens[g]
+            own = jnp.logical_and(owned >= first[g][0], owned < first[g][0] + n)
+
+            @pl.when(own)
             def _():
-                rcopy(tile, tile, z_s.at[1], z_r.at[1 + owned // HALF], (f, i * 2 + core)).start()
-
-    fan_recv(g2, 5, NZ - 1)
-    fan_sent(g2, 5, NZ - 1)
-    d_gain = jnp.sum(g2[:, 0, :], axis=0, keepdims=True)
-    d_shift = jnp.sum(g2[:, 1, :], axis=0, keepdims=True)
-    gs[0:1, :] = d_gain
-    gs[1:2, :] = d_shift
-    count = per_channel * group
-    g_mean = group_sum(gw * d_shift) / count
-    g_proj = group_sum(gw * d_gain) / count
-    out = fg.reshape(cells, ch)
-
-    @pl.loop(0, chunks)
-    def _(k):
-        at_rows = pl.ds(pl.multiple_of(k * CHUNK, CHUNK), CHUNK)
-        out[at_rows, :] = (
-            inv * (gact[at_rows, :] * gw - g_mean - xhat[at_rows, :] * g_proj)
-        ).astype(BF16)
-
-    def z_recv(h):
-        own = jnp.logical_and(owner, owned // HALF == h)
-
-        @pl.when(own)
+                rcopy(tiles(n - 1), tiles(n - 1), z_s.at[1], z_r.at[1 + g], mate).wait_recv()
+
+            @pl.when(jnp.logical_not(own))
+            def _():
+                rcopy(tiles(n), tiles(n), z_s.at[1], z_r.at[1 + g], mate).wait_recv()
+
+        def come(piece, sem):
+            rcopy(piece, piece, ag_s.at[0], sem, mate).wait_recv()
+
+        def forward(piece):
+            rcopy(piece, piece, fw_s.at[0], fw_r.at[0], mate).start()
+
+        def out_row(g, h, at):
+            return out_taps(g, h).at[:, at] if h == 0 else out_taps(g, h).at[:, :, at]
+
+        def behind(v, i):
+            return lax.rem(v - i + NX, NX)
+
+        for g in range(2):
+            z_recv(g)
+            for h in range(2):
+                piece = out_taps(g, h).at[:, x, y]
+                for i in (2, 1, 3):
+                    rcopy(piece, piece, ag_s.at[g], ag_r1.at[g, h, i - 1], late_dev(h, i)).start()
+        for g in range(2):
+            for h in range(2):
+                mine = out_row(g, h, early[h])
+                for i in (1, 3, 2):
+                    come(mine.at[:, behind(late[h], i)], ag_r1.at[g, h, i - 1])
+                forward(mine)
+                for i in (2, 1, 3):
+                    rcopy(mine, mine, ag_s.at[g], ag_r2.at[g, h, i - 1], early_dev(h, i)).start()
+        for g in range(2):
+            for i in (1, 3, 2):
+                for h in range(2):
+                    theirs = out_row(g, h, behind(early[h], i))
+                    come(theirs, ag_r2.at[g, h, i - 1])
+                    forward(theirs)
+
+        @pl.when(owner)
         def _():
-            rcopy(tiles(HALF - 1), tiles(HALF - 1), z_s.at[1], z_r.at[1 + h], mate).wait_recv()
-
-        @pl.when(jnp.logical_not(own))
+            rcopy(tiles(NZ - 1), tiles(NZ - 1), z_s.at[1], z_r.at[0], mate).wait_send()
+            rcopy(tiles(share - 1), tiles(share - 1), z_s.at[0], z_r.at[0], mate).wait_send()
+
+        @pl.when(jnp.logical_not(owner))
         def _():
-            rcopy(tiles(HALF), tiles(HALF), z_s.at[1], z_r.at[1 + h], mate).wait_recv()
-
-    def behind(v, n):
-        return [lax.rem(v - i + n, n) for i in range(1, n)]
-
-    xb, yb = behind(x, NX), behind(y, NY)
-
-    def put(piece, sem, dev):
-        rcopy(piece, piece, ag_s.at[0], sem, dev).start()
-
-    def come(piece, sem):
-        rcopy(piece, piece, ag_s.at[0], sem, mate).wait_recv()
-
-    def forward(piece):
-        rcopy(piece, piece, fw_s.at[0], fw_r.at[0], mate).start()
-
-    places = [[(x, yy) for yy in [y] + yb], [(xx, y) for xx in [x] + xb]]
-    first_devs, second_devs = [ydevs, xdevs], [xdevs, ydevs]
-    for p in range(NX):
-        for h in range(2):
-            piece = out_piece(h, *places[h][p])
-            if p == 0:
-                z_recv(h)
-                for i, dev in enumerate(first_devs[h]):
-                    put(piece, ag_r1.at[h, i], dev)
-            else:
-                come(piece, ag_r1.at[h, p - 1])
-            for i, dev in enumerate(second_devs[h]):
-                put(piece, ag_r2.at[h, p, i], dev)
-            forward(piece)
-    for p in range(NX):
-        for i in (0, 2, 1):
-            for h in range(2):
-                px, py = places[h][p]
-                piece = out_piece(0, xb[i], py) if h == 0 else out_piece(1, px, yb[i])
-                come(piece, ag_r2.at[h, p, i])
-                forward(piece)
-
-    @pl.when(owner)
-    def _():
-        rcopy(tiles(NZ - 1), tiles(NZ - 1), z_s.at[1], z_r.at[0], mate).wait_send()
-        rcopy(tiles(2 * HALF - 1), tiles(2 * HALF - 1), z_s.at[0], z_r.at[0], mate).wait_send()
-
-    @pl.when(jnp.logical_not(owner))
-    def _():
-        rcopy(tiles(2 * HALF), tiles(2 * HALF), z_s.at[0], z_r.at[0], mate).wait_send()
-
-    rcopy(sent, sent, ag_s.at[0], ag_r1.at[0, 0], mate).wait_send()
-    full = gk.at[pl.ds(share, 2 * HALF)]
-    rcopy(full, full, fw_s.at[0], fw_r.at[0], mate).wait()
+            rcopy(tiles(share), tiles(share), z_s.at[0], z_r.at[0], mate).wait_send()
+
+        for g in range(2):
+            rcopy(sent[g], sent[g], ag_s.at[g], ag_r1.at[g, 0, 0], mate).wait_send()
+        full = gk.at[pl.ds(base, share)]
+        rcopy(full, full, fw_s.at[0], fw_r.at[0], mate).wait_send()
+        theirs = gk.at[pl.ds(BASE[1 - who], SHARE[1 - who])]
+        rcopy(theirs, theirs, fw_s.at[0], fw_r.at[0], mate).wait_recv()
+
+    for who in range(2):
+        pl.when(core == who)(functools.partial(finish, who))
 
 
 def place(fg, gk, gs, fg_o, gk_o, gain_o, shift_o, sem):
@@ -455,7 +480,7 @@
         functools.partial(body, stop),
         out_shape=(
             pltpu.VMEM(features.shape, BF16),
-            pltpu.VMEM((4 * HALF, NX, NY) + tile, F32),
+            pltpu.VMEM((sum(SHARE), NX, NY) + tile, F32),
             pltpu.VMEM((2, ch), F32),
         ),
         in_specs=[hbm] * 5,
@@ -476,18 +501,16 @@
             pltpu.VMEM((2, 2, ch), F32),
             pltpu.VMEM((NF, 2, ch), F32),
             pltpu.VMEM((NZ, 2, ch), F32),
-            pltpu.VMEM((2, NX, NY, HALF) + tile, F32),
-            pltpu.VMEM((NY, 3, HALF) + tile, F32),
-            pltpu.VMEM((NX, 3, HALF) + tile, F32),
-            pltpu.VMEM((3, HALF) + tile, F32),
-            pltpu.VMEM((3, HALF) + tile, F32),
-            pltpu.VMEM((2 * HALF,) + tile, F32),
+            *(pltpu.VMEM((2, NX, NY, n) + tile, F32) for of in LENS for n in of),
+            *(pltpu.VMEM((2, 3, NX, n) + tile, F32) for of in LENS for n in of),
+            *(pltpu.VMEM((2, 3, n) + tile, F32) for of in LENS for n in of),
+            pltpu.VMEM((NZ,) + tile, F32),
             pltpu.VMEM((NZ,) + tile, F32),
             dma((5,)), dma((8,)), dma((8,)),
             dma((6,)), dma((6,)),
-            dma((1,)), dma((2, NX)), dma((2,)),
+            dma((2,)), dma((2, 2)), dma((2, 2)),
             dma((2,)), dma((3,)),
-            dma((1,)), dma((2, 3)), dma((2, NX, 3)),
+            dma((2,)), dma((2, 2, 3)), dma((2, 2, 3)),
             dma((1,)), dma((1,)),
             pltpu.SemaphoreType.REGULAR,
         ],

time: 66.2 us -> 64.6 us (0.976)
  Pallas kernels: 65.4 us -> 63.8 us
    pallas_call x1, Pallas kernels: 64.1 us -> 62.5 us  [call(): pl.pallas_call(functools.partial(body, stop), out_shape=(pltpu.VMEM(featu...]
where the time goes in v7:
time: 64.6 us; the launch traced here: 64.4 us
  Pallas kernels  63.8 us (99%)
    pallas_call x1, Pallas kernels, call(): pl.pallas_call(functools.partial(body, stop), out_shape=(pltpu.VMEM(featu...  62.5 us
    pallas_call x1, Pallas kernels, on_device(): pl.pallas_call(place, out_shape=(jax.ShapeDtypeStruct(features.shape, BF1...  1.3 us

profile of v7, /device:TPU:1, one launch (start us, length us, event | category | flops | bytes accessed | tf_op | source)
XLA Modules:
  0.0 64.4 jit_solution(15615751308590199780)
XLA Ops:
  0.6 62.5 %shard_map.84 = (bf16[2,6,64,128]{3,2,1,0:T(8,128)(2,1)S(1)}, f32[28,4,4,8,128]{4,3,2,1,0:T(8,128)S(1)}, f32[2,128]{1,0:T(2,128)S(1)}) custom-call(bf16[2,6,64,128]{3,2,1,0:T(8,128)(2,1)} %feat_h.1, f32[1,128]{1,0:T(1,128)} %bitcast.7, f32[1,128]{1,0:T(1,128)} %bitcast.8, bf16[27,128,128]{2,1,0:T(8,128)(2,1)} %bitcast.6, bf16[2,6,64,128]{3,2,1,0:T(8,128)(2,1)} %cot_h.1), custom_call_target="tpu_custom_call" | custom-call | tf_op jit(solution)/shard_map/pallas_call | solution.py:479
  63.1 1.3 %shard_map.85 = (bf16[2,6,64,128]{3,2,1,0:T(8,128)(2,1)}, f32[27,4,4,8,128]{4,3,2,1,0:T(8,128)}, f32[1,128]{1,0:T(1,128)}, f32[1,128]{1,0:T(1,128)}) custom-call(bf16[2,6,64,128]{3,2,1,0:T(8,128)(2,1)S(1)} %get-tuple-element.11.fg, f32[28,4,4,8,128]{4,3,2,1,0:T(8,128)S(1)} %get-tuple-element.12.gk, f32[2,128]{1,0:T(2,128)S(1)} %get-tuple-element.13.gs), custom_call_target="tpu_custom_call" | custom-call | tf_op jit(solution)/shard_map/pallas_call | solution.py:539

commit v8 on v7

--- a/solution.py
+++ b/solution.py
@@ -15,14 +15,14 @@
 NZ = 16
 NF = NX * NY
 LAST = 26
-LENS = ((3, 3), (4, 4))
-SHARE = tuple(2 * sum(n) for n in LENS)
+LENS = (((3, 3), (3, 3)), ((4, 4), (4, 3)))
+SHARE = tuple(sum(map(sum, of)) for of in LENS)
 BASE = (0, SHARE[0])
-FROM = tuple(((0, n), (2 * n, 2 * n + m)) for n, m in LENS)
+FROM = tuple(((0, p[0]), (sum(p), sum(p) + q[0])) for p, q in LENS)
+FIRST = (11, 9)
 F32 = jnp.float32
 BF16 = jnp.bfloat16
 CHUNK = 128
-FIRST = NZ // 2 + 1
 REACH = NZ // 4
 
 
@@ -44,8 +44,8 @@
     fg, gk, gs,
     fx, gain, bias, w, ext, cotx, gact, xhat, feat_t, act_t,
     s1, s2, g0, g1, g2,
-    part00, part01, part10, part11, ra00, ra01, ra10, ra11, rb00, rb01, rb10, rb11, zsrc, rz,
-    load_s, halo_s, halo_r, sm_s, sm_r, rs_s, rs_r1, rs_r2, z_s, z_r, ag_s, ag_r1, ag_r2, fw_s, fw_r, known,
+    zsrc, rz,
+    load_s, halo_s, halo_r, sm_s, sm_r, rs_s, rs_r1, rs_r2, z_s, z_r, ag_s, ag_r1, ag_r2, fw_s, fw_r, known, *bufs,
 ):
     f, t = lax.axis_index("frame"), lax.axis_index("tile")
     y, x = f // NX, lax.rem(f, NX)
@@ -247,9 +247,10 @@
         act_t[k] = (nrm * (1.0 / (1.0 + jnp.exp(-nrm)))).astype(BF16)
 
     def finish(who):
-        parts = [[part00, part01], [part10, part11]][who]
-        ra = [[ra00, ra01], [ra10, ra11]][who]
-        rb = [[rb00, rb01], [rb10, rb11]][who]
+        parts, ra, rb = (
+            [[bufs[8 * kind + 4 * who + 2 * g + h] for h in range(2)] for g in range(2)]
+            for kind in range(3)
+        )
         lens, first, share, base = LENS[who], FROM[who], SHARE[who], BASE[who]
         early, late = [x, y], [y, x]
 
@@ -260,27 +261,28 @@
             return early_dev(1 - h, i)
 
         def row(ref, h, at):
-            return ref.at[h, at] if h == 0 else ref.at[h, :, at]
+            return ref.at[at] if h == 0 else ref.at[:, at]
 
         acts = jnp.concatenate([act_t[i] for i in range(2 * chunks)], axis=1)
 
         def first_stage(g):
-            for j in range(lens[g]):
+            for j in range(max(lens[g])):
+                halves = [h for h in range(2) if j < lens[g][h]]
                 got = []
-                for h in range(2):
-                    tap = min(base + first[g][h] + j, LAST)
+                for h in halves:
+                    tap = base + first[g][h] + j
                     a, b, e = tap // 9, tap // 3 % 3, tap % 3
                     got.append(
                         cotx[e, pl.ds(2 - a, frames), pl.ds(2 - b, 2 * rows)].reshape(2 * cells, ch)
                     )
                 out = jnp.dot(acts, jnp.concatenate(got, axis=1), preferred_element_type=F32)
-                for h in range(2):
-                    parts[g][h, :, :, j] = out[:, h * ch : (h + 1) * ch].reshape(NX, NY, 8, ch)
+                for n, h in enumerate(halves):
+                    parts[g][h][:, :, j] = out[:, n * ch : (n + 1) * ch].reshape(NX, NY, 8, ch)
             for h in range(2):
                 for i in (2, 1, 3):
                     to = lax.rem(early[h] + i, NX)
                     rcopy(
-                        row(parts[g], h, to), ra[g].at[h, i - 1], rs_s.at[g], rs_r1.at[g, h], early_dev(h, i)
+                        row(parts[g][h], h, to), ra[g][h].at[i - 1], rs_s.at[g, h], rs_r1.at[g, h], early_dev(h, i)
                     ).start()
 
         first_stage(0)
@@ -324,25 +326,25 @@
 
         def second_stage(g):
             for h in range(2):
-                got = ra[g].at[h]
-                rcopy(got, got, rs_s.at[g], rs_r1.at[g, h], mate).wait_recv()
-                mine = row(parts[g], h, early[h])
+                got = ra[g][h]
+                rcopy(got, got, rs_s.at[g, h], rs_r1.at[g, h], mate).wait_recv()
+                mine = row(parts[g][h], h, early[h])
                 mine[...] += got[0] + got[1] + got[2]
                 for i in (2, 1, 3):
                     rcopy(
-                        mine.at[lax.rem(late[h] + i, NX)], rb[g].at[h, i - 1], rs_s.at[g], rs_r2.at[g, h],
+                        mine.at[lax.rem(late[h] + i, NX)], rb[g][h].at[i - 1], rs_s.at[g, h], rs_r2.at[g, h],
                         late_dev(h, i),
                     ).start()
 
         def z_stage(g):
             for h in range(2):
-                got = rb[g].at[h]
-                rcopy(got, got, rs_s.at[g], rs_r2.at[g, h], mate).wait_recv()
-                zsrc[first[g][h] : first[g][h] + lens[g]] = parts[g][h, x, y] + (got[0] + got[1] + got[2])
+                got = rb[g][h]
+                rcopy(got, got, rs_s.at[g, h], rs_r2.at[g, h], mate).wait_recv()
+                zsrc[first[g][h] : first[g][h] + lens[g][h]] = parts[g][h][x, y] + (got[0] + got[1] + got[2])
             for to, dev in zip(zs, zdevs):
-                q = lax.rem(to + NZ - FIRST, NZ)
-
-                @pl.when(jnp.logical_and(q >= first[g][0], q < first[g][0] + 2 * lens[g]))
+                q = lax.rem(to + NZ - FIRST[who], NZ)
+
+                @pl.when(jnp.logical_and(q >= first[g][0], q < first[g][0] + sum(lens[g])))
                 def _():
                     rcopy(zsrc.at[q], rz.at[z], z_s.at[0], z_r.at[0], dev).start()
 
@@ -350,16 +352,20 @@
         second_stage(1)
         z_stage(0)
         z_stage(1)
-        owned = lax.rem(z + NZ - FIRST, NZ)
+        owned = lax.rem(z + NZ - FIRST[who], NZ)
         owner = owned < share
 
         pass_on(g1, 4, NF - 1, g2, z, zdevs)
-        sent = [parts[g].reshape(2 * NX * NY, lens[g], 8, ch).at[pl.ds(0, 30)] for g in range(2)]
+        sent = [
+            [parts[g][h].reshape(NX * NY, lens[g][h], 8, ch).at[pl.ds(0, NX * NY - 1)] for h in range(2)]
+            for g in range(2)
+        ]
         for g in range(2):
-            rcopy(sent[g], sent[g], rs_s.at[g], rs_r2.at[g, 0], mate).wait_send()
+            for h in range(2):
+                rcopy(sent[g][h], sent[g][h], rs_s.at[g, h], rs_r2.at[g, h], mate).wait_send()
 
         def out_taps(g, h):
-            return gk.at[pl.ds(base + first[g][h], lens[g])]
+            return gk.at[pl.ds(base + first[g][h], lens[g][h])]
 
         def tiles(n):
             return rz.at[pl.ds(0, n)]
@@ -392,7 +398,7 @@
             ).astype(BF16)
 
         def z_recv(g):
-            n = 2 * lens[g]
+            n = sum(lens[g])
             own = jnp.logical_and(owned >= first[g][0], owned < first[g][0] + n)
 
             @pl.when(own)
@@ -404,7 +410,7 @@
                 rcopy(tiles(n), tiles(n), z_s.at[1], z_r.at[1 + g], mate).wait_recv()
 
         def come(piece, sem):
-            rcopy(piece, piece, ag_s.at[0], sem, mate).wait_recv()
+            rcopy(piece, piece, ag_s.at[0, 0], sem, mate).wait_recv()
 
         def forward(piece):
             rcopy(piece, piece, fw_s.at[0], fw_r.at[0], mate).start()
@@ -420,7 +426,7 @@
             for h in range(2):
                 piece = out_taps(g, h).at[:, x, y]
                 for i in (2, 1, 3):
-                    rcopy(piece, piece, ag_s.at[g], ag_r1.at[g, h, i - 1], late_dev(h, i)).start()
+                    rcopy(piece, piece, ag_s.at[g, h], ag_r1.at[g, h, i - 1], late_dev(h, i)).start()
         for g in range(2):
             for h in range(2):
                 mine = out_row(g, h, early[h])
@@ -428,7 +434,7 @@
                     come(mine.at[:, behind(late[h], i)], ag_r1.at[g, h, i - 1])
                 forward(mine)
                 for i in (2, 1, 3):
-                    rcopy(mine, mine, ag_s.at[g], ag_r2.at[g, h, i - 1], early_dev(h, i)).start()
+                    rcopy(mine, mine, ag_s.at[g, h], ag_r2.at[g, h, i - 1], early_dev(h, i)).start()
         for g in range(2):
             for i in (1, 3, 2):
                 for h in range(2):
@@ -446,7 +452,8 @@
             rcopy(tiles(share), tiles(share), z_s.at[0], z_r.at[0], mate).wait_send()
 
         for g in range(2):
-            rcopy(sent[g], sent[g], ag_s.at[g], ag_r1.at[g, 0, 0], mate).wait_send()
+            for h in range(2):
+                rcopy(sent[g][h], sent[g][h], ag_s.at[g, h], ag_r1.at[g, h, 0], mate).wait_send()
         full = gk.at[pl.ds(base, share)]
         rcopy(full, full, fw_s.at[0], fw_r.at[0], mate).wait_send()
         theirs = gk.at[pl.ds(BASE[1 - who], SHARE[1 - who])]
@@ -501,18 +508,22 @@
             pltpu.VMEM((2, 2, ch), F32),
             pltpu.VMEM((NF, 2, ch), F32),
             pltpu.VMEM((NZ, 2, ch), F32),
-            *(pltpu.VMEM((2, NX, NY, n) + tile, F32) for of in LENS for n in of),
-            *(pltpu.VMEM((2, 3, NX, n) + tile, F32) for of in LENS for n in of),
-            *(pltpu.VMEM((2, 3, n) + tile, F32) for of in LENS for n in of),
             pltpu.VMEM((NZ,) + tile, F32),
             pltpu.VMEM((NZ,) + tile, F32),
             dma((5,)), dma((8,)), dma((8,)),
             dma((6,)), dma((6,)),
-            dma((2,)), dma((2, 2)), dma((2, 2)),
+            dma((2, 2)), dma((2, 2)), dma((2, 2)),
             dma((2,)), dma((3,)),
-            dma((2,)), dma((2, 2, 3)), dma((2, 2, 3)),
+            dma((2, 2)), dma((2, 2, 3)), dma((2, 2, 3)),
             dma((1,)), dma((1,)),
             pltpu.SemaphoreType.REGULAR,
+            *(
+                pltpu.VMEM(dims + (n,) + tile, F32)
+                for dims in ((NX, NY), (3, NX), (3,))
+                for of in LENS
+                for pair in of
+                for n in pair
+            ),
         ],
         compiler_params=pltpu.CompilerParams(
             collective_id=cid, has_side_effects=True, vmem_limit_bytes=24 * 2**20

time: 64.6 us -> 64.2 us (level)
  no operation moved by 1% of the time
where the time goes in v8:
time: 64.2 us; the launch traced here: 64.1 us
  Pallas kernels  63.5 us (99%)
    pallas_call x1, Pallas kernels, call(): pl.pallas_call(functools.partial(body, stop), out_shape=(pltpu.VMEM(featu...  62.2 us
    pallas_call x1, Pallas kernels, on_device(): pl.pallas_call(place, out_shape=(jax.ShapeDtypeStruct(features.shape, BF1...  1.3 us

profile of v8, /device:TPU:1, one launch (start us, length us, event | category | flops | bytes accessed | tf_op | source)
XLA Modules:
  0.0 64.1 jit_solution(14250390831263693516)
XLA Ops:
  0.6 62.2 %shard_map.84 = (bf16[2,6,64,128]{3,2,1,0:T(8,128)(2,1)S(1)}, f32[27,4,4,8,128]{4,3,2,1,0:T(8,128)S(1)}, f32[2,128]{1,0:T(2,128)S(1)}) custom-call(bf16[2,6,64,128]{3,2,1,0:T(8,128)(2,1)} %feat_h.1, f32[1,128]{1,0:T(1,128)} %bitcast.7, f32[1,128]{1,0:T(1,128)} %bitcast.8, bf16[27,128,128]{2,1,0:T(8,128)(2,1)} %bitcast.6, bf16[2,6,64,128]{3,2,1,0:T(8,128)(2,1)} %cot_h.1), custom_call_target="tpu_custom_call" | custom-call | tf_op jit(solution)/shard_map/pallas_call | solution.py:486
  62.8 1.3 %shard_map.85 = (bf16[2,6,64,128]{3,2,1,0:T(8,128)(2,1)}, f32[27,4,4,8,128]{4,3,2,1,0:T(8,128)}, f32[1,128]{1,0:T(1,128)}, f32[1,128]{1,0:T(1,128)}) custom-call(bf16[2,6,64,128]{3,2,1,0:T(8,128)(2,1)S(1)} %get-tuple-element.11.fg, f32[27,4,4,8,128]{4,3,2,1,0:T(8,128)S(1)} %get-tuple-element.12.gk, f32[2,128]{1,0:T(2,128)S(1)} %get-tuple-element.13.gs), custom_call_target="tpu_custom_call" | custom-call | tf_op jit(solution)/shard_map/pallas_call | solution.py:550

commit v9 on v8

--- a/solution.py
+++ b/solution.py
@@ -43,7 +43,7 @@
     feat_h, gain_h, bias_h, w_h, cot_h,
     fg, gk, gs,
     fx, gain, bias, w, ext, cotx, gact, xhat, feat_t, act_t,
-    s1, s2, g0, g1, g2,
+    s1, s2, s3, g0, g1, g2,
     zsrc, rz,
     load_s, halo_s, halo_r, sm_s, sm_r, rs_s, rs_r1, rs_r2, z_s, z_r, ag_s, ag_r1, ag_r2, fw_s, fw_r, known, *bufs,
 ):
@@ -120,8 +120,12 @@
         many = buf.at[pl.ds(0, n)]
         rcopy(many, many, sm_s.at[k], sm_r.at[k], mate).wait_send()
 
-    for dev in fboth:
+    def send_moments(dev):
         rcopy(s1.at[core, f], s1.at[core, f], sm_s.at[1], sm_r.at[1], dev).start()
+
+    pl.when(core == 0)(lambda: send_moments(mate))
+    for dev in fdevs:
+        send_moments((dev[0], z * 2 + 1))
     for dev in edge:
         pl.semaphore_signal(known, inc=1, device_id=dev, device_id_type=MESH)
     block = ext.at[0:2, own_rows]
@@ -170,13 +174,19 @@
     for c in rims:
         c.start()
 
-    s1 = s1.reshape(2 * NF, 2, ch)
-    fan_recv(s1, 1, 2 * NF - 1)
-    avg, m2 = combine(s1, float(cells))
-    s2[z, 0:1, :] = avg
-    s2[z, 1:2, :] = m2
     pl.semaphore_wait(known, len(edge))
-    fan(s2, z, zdevs, 2)
+
+    @pl.when(core == 1)
+    def _():
+        moments = s1.reshape(2 * NF, 2, ch)
+        fan_recv(moments, 1, 2 * NF - 1)
+        avg, m2 = combine(moments, float(cells))
+        s2[z, 0:1, :] = avg
+        s2[z, 1:2, :] = m2
+        fan(s2, z, zdevs, 2)
+        fan_sent(moments, 1, NF - 1)
+
+    pl.when(core == 0)(lambda: fan_sent(s1.reshape(2 * NF, 2, ch), 1, NF))
 
     to_before.wait_recv()
     relay = rcopy(later, later, halo_s.at[7], halo_r.at[7], mate)
@@ -197,7 +207,6 @@
     for c in rims:
         c.wait()
     relay.wait()
-    fan_sent(s1, 1, 2 * NF - 1)
 
     @pl.when(f == NF - 1)
     def _():
@@ -222,11 +231,20 @@
         return jnp.broadcast_to(v, (CHUNK, ch)).T
 
     bias_t = down(bw)
-    fan_recv(s2, 2, NZ - 1)
-    fan_sent(s2, 2, NZ - 1)
-    if stop == 2:
-        return
-    avg, m2 = combine(s2, float(cells * 2 * NF))
+    to_mate = rcopy(s3, s3, sm_s.at[0], sm_r.at[0], mate)
+
+    @pl.when(core == 1)
+    def _():
+        fan_recv(s2, 2, NZ - 1)
+        avg, m2 = combine(s2, float(cells * 2 * NF))
+        s3[0:1, :] = avg
+        s3[1:2, :] = m2
+        to_mate.start()
+        fan_sent(s2, 2, NZ - 1)
+        to_mate.wait_send()
+
+    pl.when(core == 0)(to_mate.wait_recv)
+    avg, m2 = s3[0:1, :], s3[1:2, :]
     per_channel = float(cells * 2 * NF * NZ)
     group = ch // GROUPS
     g_avg = group_sum(avg) / group
@@ -505,6 +523,7 @@
             pltpu.VMEM((2 * cells // CHUNK, ch, CHUNK), BF16),
             pltpu.VMEM((2, NF, 2, ch), F32),
             pltpu.VMEM((NZ, 2, ch), F32),
+            pltpu.VMEM((2, ch), F32),
             pltpu.VMEM((2, 2, ch), F32),
             pltpu.VMEM((NF, 2, ch), F32),
             pltpu.VMEM((NZ, 2, ch), F32),

time: 64.2 us -> 64 us (level)
  no operation moved by 1% of the time
where the time goes in v9:
time: 64 us; the launch traced here: 63.9 us
  Pallas kernels  63.3 us (99%)
  between operations  0.64 us (1%)
    pallas_call x1, Pallas kernels, call(): pl.pallas_call(functools.partial(body, stop), out_shape=(pltpu.VMEM(featu...  62 us
    pallas_call x1, Pallas kernels, on_device(): pl.pallas_call(place, out_shape=(jax.ShapeDtypeStruct(features.shape, BF1...  1.3 us

profile of v9, /device:TPU:1, one launch (start us, length us, event | category | flops | bytes accessed | tf_op | source)
XLA Modules:
  0.0 63.9 jit_solution(2596491553096412843)
XLA Ops:
  0.6 62.0 %shard_map.84 = (bf16[2,6,64,128]{3,2,1,0:T(8,128)(2,1)S(1)}, f32[27,4,4,8,128]{4,3,2,1,0:T(8,128)S(1)}, f32[2,128]{1,0:T(2,128)S(1)}) custom-call(bf16[2,6,64,128]{3,2,1,0:T(8,128)(2,1)} %feat_h.1, f32[1,128]{1,0:T(1,128)} %bitcast.7, f32[1,128]{1,0:T(1,128)} %bitcast.8, bf16[27,128,128]{2,1,0:T(8,128)(2,1)} %bitcast.6, bf16[2,6,64,128]{3,2,1,0:T(8,128)(2,1)} %cot_h.1), custom_call_target="tpu_custom_call" | custom-call | tf_op jit(solution)/shard_map/pallas_call | solution.py:504
  62.6 1.3 %shard_map.85 = (bf16[2,6,64,128]{3,2,1,0:T(8,128)(2,1)}, f32[27,4,4,8,128]{4,3,2,1,0:T(8,128)}, f32[1,128]{1,0:T(1,128)}, f32[1,128]{1,0:T(1,128)}) custom-call(bf16[2,6,64,128]{3,2,1,0:T(8,128)(2,1)S(1)} %get-tuple-element.11.fg, f32[27,4,4,8,128]{4,3,2,1,0:T(8,128)S(1)} %get-tuple-element.12.gk, f32[2,128]{1,0:T(2,128)S(1)} %get-tuple-element.13.gs), custom_call_target="tpu_custom_call" | custom-call | tf_op jit(solution)/shard_map/pallas_call | solution.py:569

commit v10 on v9

--- a/solution.py
+++ b/solution.py
@@ -340,7 +340,6 @@
             fan(to, me, devs, k + 1)
             fan_sent(buf, k, n)
 
-        pass_on(g0, 3, 1, g1, f, fdevs)
 
         def second_stage(g):
             for h in range(2):
@@ -367,6 +366,7 @@
                     rcopy(zsrc.at[q], rz.at[z], z_s.at[0], z_r.at[0], dev).start()
 
         second_stage(0)
+        pass_on(g0, 3, 1, g1, f, fdevs)
         second_stage(1)
         z_stage(0)
         z_stage(1)

time: 64 us -> 63.9 us (level)
  no operation moved by 1% of the time
where the time goes in v10:
time: 63.9 us; the launch traced here: 63.7 us
  Pallas kernels  63.1 us (99%)
  between operations  0.64 us (1%)
    pallas_call x1, Pallas kernels, call(): pl.pallas_call(functools.partial(body, stop), out_shape=(pltpu.VMEM(featu...  61.8 us
    pallas_call x1, Pallas kernels, on_device(): pl.pallas_call(place, out_shape=(jax.ShapeDtypeStruct(features.shape, BF1...  1.3 us

profile of v10, /device:TPU:1, one launch (start us, length us, event | category | flops | bytes accessed | tf_op | source)
XLA Modules:
  0.0 63.7 jit_solution(1915553122027277538)
XLA Ops:
  0.6 61.8 %shard_map.84 = (bf16[2,6,64,128]{3,2,1,0:T(8,128)(2,1)S(1)}, f32[27,4,4,8,128]{4,3,2,1,0:T(8,128)S(1)}, f32[2,128]{1,0:T(2,128)S(1)}) custom-call(bf16[2,6,64,128]{3,2,1,0:T(8,128)(2,1)} %feat_h.1, f32[1,128]{1,0:T(1,128)} %bitcast.7, f32[1,128]{1,0:T(1,128)} %bitcast.8, bf16[27,128,128]{2,1,0:T(8,128)(2,1)} %bitcast.6, bf16[2,6,64,128]{3,2,1,0:T(8,128)(2,1)} %cot_h.1), custom_call_target="tpu_custom_call" | custom-call | tf_op jit(solution)/shard_map/pallas_call | solution.py:504
  62.4 1.3 %shard_map.85 = (bf16[2,6,64,128]{3,2,1,0:T(8,128)(2,1)}, f32[27,4,4,8,128]{4,3,2,1,0:T(8,128)}, f32[1,128]{1,0:T(1,128)}, f32[1,128]{1,0:T(1,128)}) custom-call(bf16[2,6,64,128]{3,2,1,0:T(8,128)(2,1)S(1)} %get-tuple-element.11.fg, f32[27,4,4,8,128]{4,3,2,1,0:T(8,128)S(1)} %get-tuple-element.12.gk, f32[2,128]{1,0:T(2,128)S(1)} %get-tuple-element.13.gs), custom_call_target="tpu_custom_call" | custom-call | tf_op jit(solution)/shard_map/pallas_call | solution.py:569
